TPU v7x, 32 devices: a whole 2x2x4 slice. The times are simulated.
32 devices in a mesh: sec: 4 (over z), row: 2 (over x), inner: 4 (over y, core).
Axes of the slice: x: 2, y: 2, z: 4, core: 2. Of those that a mesh axis runs over, the one named last changes fastest.
Arguments:
- amplitudes: bfloat16 [256, 4, 16384], P('row', 'inner'), may hold values from -6 to 6
- hole_ladder: bfloat16 [256, 256], P('row'), may hold values from -0.375 to 0.375
- bare_integrals: bfloat16 [256, 4, 16384], P('row', 'inner', 'sec'), may hold values from -6 to 6
- ladder_tiles: bfloat16 [1024, 512, 128], P('sec', 'inner'), may hold values from -0.1875 to 0.1875
- ladder_source: int32 [1024, 4], P('sec', 'inner'), may hold values from 0 to 127
- ladder_target: int32 [1024, 4], P('sec', 'inner'), may hold values from 0 to 127
- ladder_live: int32 [4, 4], P('sec', 'inner'), may hold values from 64 to 256, as said below
- cycle_tiles: bfloat16 [128, 512, 128], P('sec', 'inner'), may hold values from -0.5 to 0.5
- cycle_source: int32 [128, 4], P('sec', 'inner'), may hold values from 0 to 63
- cycle_target: int32 [128, 4], P('sec', 'inner'), may hold values from 0 to 127
- gap_rows: int32 [256], P('row'), may hold values from 512 to 2047
- gap_columns: int32 [4, 16384], P('inner', 'sec'), may hold values from 512 to 2047
Outputs:
- updated: bfloat16 [256, 4, 16384], P('row', 'inner', 'sec')
Inputs may be any that keep to these rules, and one draw needn't show every extreme that they name: Slots from ladder_live on are padding and carry no term; some section and quarter has all 256 slots live in every draw.
All inputs are finite; a program needn't handle non-finite values.
Results may differ from a plain program's by a relative error of at most 0.0095.
Values may be sent and summed in bfloat16 or wider, within the bound.
A program may use at most 128 MiB of HBM per device.

v0:
```python
import jax
import jax.numpy as jnp
from jax import lax
from jax.sharding import PartitionSpec as P

TILE = 128
TILE_GROUP = 16
PANEL = 2048


def apply_tiles(totals, source_blocks, tiles, sources, targets, live_count, turn_count):

    def one_turn(turn_index, running):
        offset = turn_index * TILE_GROUP
        group_tiles = lax.dynamic_slice_in_dim(tiles, offset, TILE_GROUP, 0)
        group_sources = lax.dynamic_slice_in_dim(sources, offset, TILE_GROUP, 0)
        group_targets = lax.dynamic_slice_in_dim(targets, offset, TILE_GROUP, 0)
        picked = jnp.take(source_blocks, group_sources, axis=1)
        contribution = jnp.einsum(
            "rtk,tkc->rtc", picked, group_tiles, preferred_element_type=jnp.float32
        )
        keep_mask = (offset + jnp.arange(TILE_GROUP) < live_count).astype(jnp.float32)
        contribution = contribution * keep_mask[None, :, None]
        return running.at[:, group_targets].add(contribution)

    return lax.fori_loop(0, turn_count, one_turn, totals)


def per_device(
    amplitudes,
    hole_ladder,
    bare_integrals,
    ladder_tiles,
    ladder_source,
    ladder_target,
    ladder_live,
    cycle_tiles,
    cycle_source,
    cycle_target,
    gap_rows,
    gap_columns,
):
    row_count = amplitudes.shape[0]
    quarter_width = amplitudes.shape[2]
    block_count = quarter_width // TILE
    owned_width = bare_integrals.shape[2]
    own_blocks = amplitudes.reshape(row_count, block_count, TILE)
    gathered_panel = lax.all_gather(amplitudes[:, :, :PANEL], "inner", axis=1, tiled=True)
    panel_blocks = gathered_panel.reshape(row_count, gathered_panel.shape[1] * PANEL // TILE, TILE)
    live_count = ladder_live[0, 0]
    totals = jnp.zeros((row_count, block_count, TILE), jnp.float32)
    totals = apply_tiles(
        totals,
        own_blocks,
        ladder_tiles,
        ladder_source[:, 0],
        ladder_target[:, 0],
        live_count,
        (live_count + TILE_GROUP - 1) // TILE_GROUP,
    )
    cycle_count = cycle_tiles.shape[0]
    totals = apply_tiles(
        totals,
        panel_blocks,
        cycle_tiles,
        cycle_source[:, 0],
        cycle_target[:, 0],
        cycle_count,
        cycle_count // TILE_GROUP,
    )
    partial_sum = totals.reshape(row_count, 1, quarter_width)
    owned_start = lax.axis_index("sec") * owned_width
    joined = lax.psum_scatter(
        partial_sum.astype(jnp.bfloat16), "sec", scatter_dimension=2, tiled=True
    ).astype(jnp.float32)
    owned_amps = lax.dynamic_slice_in_dim(amplitudes, owned_start, owned_width, 2).reshape(
        row_count, owned_width
    )
    hole_term = jnp.dot(
        hole_ladder,
        lax.all_gather(owned_amps, "row", axis=0, tiled=True),
        preferred_element_type=jnp.float32,
    )
    residual = bare_integrals[:, 0, :].astype(jnp.float32) + joined[:, 0, :] + hole_term
    denominator = (gap_rows[:, None] + gap_columns[0][None, :]).astype(jnp.float32) / 1024.0
    updated = (residual / denominator).astype(jnp.bfloat16)
    return updated.reshape(row_count, 1, owned_width)


def solution(mesh):
    in_specs = (
        P("row", "inner", None),
        P("row", None),
        P("row", "inner", "sec"),
        P("sec", "inner", None),
        P("sec", "inner"),
        P("sec", "inner"),
        P("sec", "inner"),
        P("sec", "inner", None),
        P("sec", "inner"),
        P("sec", "inner"),
        P("row"),
        P("inner", "sec"),
    )
    out_specs = P("row", "inner", "sec")
    return jax.shard_map(
        per_device, mesh=mesh, in_specs=in_specs, out_specs=out_specs, check_vma=False
    )
```

profile of v0, /device:TPU:17, one launch (start us, length us, event | category | flops | bytes accessed | tf_op | source)
XLA Modules:
  0.0 293.3 jit_solution(15001959642677245766)
XLA Ops:
  11.6 6.4 %copy.44 = bf16[128,1,16384]{0,2,1:T(8,128)(2,1)} copy(bf16[128,1,16384]{2,0,1:T(8,128)(2,1)} %param.16) | data formatting | bytes 8388608 | tf_op args[0]
  18.0 6.6 %copy.46 = bf16[128,128,128]{2,0,1:T(8,128)(2,1)} copy(bf16[128,128,128]{0,2,1:T(8,128)(2,1)} %bitcast.46) | data formatting | bytes 8388608 | tf_op jit(solution)/shard_map/while | solution.py:26
  24.6 4.3 %broadcast_in_dim.54 = f32[128,128,128]{2,0,1:T(8,128)} broadcast(f32[]{:T(128)} %constant.115.clone.1), dimensions={} | broadcast | bytes 8388612 | tf_op jit(solution)/shard_map/broadcast_in_dim | solution.py:51
  28.8 107.8 %while.23 = (s32[]{:T(128)}, f32[128,128,128]{2,0,1:T(8,128)}, s32[]{:T(128)}, s32[256]{0:T(256)S(1)}, bf16[256,128,128]{2,1,0:T(8,128)(2,1)}, /*index=5*/s32[25...) while((s32[]{:T(128)}, f32[128,128,128]{2,0,1:T(8,128)}, ...), condition=%wide.region_2.3_spmd, body=%wide.region_0.2_spmd.sunk | while | flops 67896520 | bytes 8393495 | solution.py:26
  34.5 3.3 %scatter_fusion = f32[128,128,128]{2,0,1:T(8,128)} fusion(f32[128,128,128]{2,0,1:T(8,128)} %get-tuple-element.361, s32[16]{0:T(128)S(1)} %compare_select_fusion.8, f32[16,128,128]{2,1,0:T(8,128)S(1)} %copy.56), kind=kCustom, calls=%fused_computation.2.clone.1 | custom fusion | flops 262144 | bytes 3145792 | tf_op jit(solution)/shard_map/while/body/scatter-add | solution.py:24
  43.5 3.5 %scatter_fusion = f32[128,128,128]{2,0,1:T(8,128)} fusion(f32[128,128,128]{2,0,1:T(8,128)} %get-tuple-element.361, s32[16]{0:T(128)S(1)} %compare_select_fusion.8, f32[16,128,128]{2,1,0:T(8,128)S(1)} %copy.56), kind=kCustom, calls=%fused_computation.2.clone.1 | custom fusion | flops 262144 | bytes 3145792 | tf_op jit(solution)/shard_map/while/body/scatter-add | solution.py:24
  52.6 3.4 %scatter_fusion = f32[128,128,128]{2,0,1:T(8,128)} fusion(f32[128,128,128]{2,0,1:T(8,128)} %get-tuple-element.361, s32[16]{0:T(128)S(1)} %compare_select_fusion.8, f32[16,128,128]{2,1,0:T(8,128)S(1)} %copy.56), kind=kCustom, calls=%fused_computation.2.clone.1 | custom fusion | flops 262144 | bytes 3145792 | tf_op jit(solution)/shard_map/while/body/scatter-add | solution.py:24
  61.6 3.4 %scatter_fusion = f32[128,128,128]{2,0,1:T(8,128)} fusion(f32[128,128,128]{2,0,1:T(8,128)} %get-tuple-element.361, s32[16]{0:T(128)S(1)} %compare_select_fusion.8, f32[16,128,128]{2,1,0:T(8,128)S(1)} %copy.56), kind=kCustom, calls=%fused_computation.2.clone.1 | custom fusion | flops 262144 | bytes 3145792 | tf_op jit(solution)/shard_map/while/body/scatter-add | solution.py:24
  70.6 3.4 %scatter_fusion = f32[128,128,128]{2,0,1:T(8,128)} fusion(f32[128,128,128]{2,0,1:T(8,128)} %get-tuple-element.361, s32[16]{0:T(128)S(1)} %compare_select_fusion.8, f32[16,128,128]{2,1,0:T(8,128)S(1)} %copy.56), kind=kCustom, calls=%fused_computation.2.clone.1 | custom fusion | flops 262144 | bytes 3145792 | tf_op jit(solution)/shard_map/while/body/scatter-add | solution.py:24
  79.5 3.4 %scatter_fusion = f32[128,128,128]{2,0,1:T(8,128)} fusion(f32[128,128,128]{2,0,1:T(8,128)} %get-tuple-element.361, s32[16]{0:T(128)S(1)} %compare_select_fusion.8, f32[16,128,128]{2,1,0:T(8,128)S(1)} %copy.56), kind=kCustom, calls=%fused_computation.2.clone.1 | custom fusion | flops 262144 | bytes 3145792 | tf_op jit(solution)/shard_map/while/body/scatter-add | solution.py:24
  88.5 3.4 %scatter_fusion = f32[128,128,128]{2,0,1:T(8,128)} fusion(f32[128,128,128]{2,0,1:T(8,128)} %get-tuple-element.361, s32[16]{0:T(128)S(1)} %compare_select_fusion.8, f32[16,128,128]{2,1,0:T(8,128)S(1)} %copy.56), kind=kCustom, calls=%fused_computation.2.clone.1 | custom fusion | flops 262144 | bytes 3145792 | tf_op jit(solution)/shard_map/while/body/scatter-add | solution.py:24
  97.5 3.4 %scatter_fusion = f32[128,128,128]{2,0,1:T(8,128)} fusion(f32[128,128,128]{2,0,1:T(8,128)} %get-tuple-element.361, s32[16]{0:T(128)S(1)} %compare_select_fusion.8, f32[16,128,128]{2,1,0:T(8,128)S(1)} %copy.56), kind=kCustom, calls=%fused_computation.2.clone.1 | custom fusion | flops 262144 | bytes 3145792 | tf_op jit(solution)/shard_map/while/body/scatter-add | solution.py:24
  106.4 3.3 %scatter_fusion = f32[128,128,128]{2,0,1:T(8,128)} fusion(f32[128,128,128]{2,0,1:T(8,128)} %get-tuple-element.361, s32[16]{0:T(128)S(1)} %compare_select_fusion.8, f32[16,128,128]{2,1,0:T(8,128)S(1)} %copy.56), kind=kCustom, calls=%fused_computation.2.clone.1 | custom fusion | flops 262144 | bytes 3145792 | tf_op jit(solution)/shard_map/while/body/scatter-add | solution.py:24
  115.4 3.4 %scatter_fusion = f32[128,128,128]{2,0,1:T(8,128)} fusion(f32[128,128,128]{2,0,1:T(8,128)} %get-tuple-element.361, s32[16]{0:T(128)S(1)} %compare_select_fusion.8, f32[16,128,128]{2,1,0:T(8,128)S(1)} %copy.56), kind=kCustom, calls=%fused_computation.2.clone.1 | custom fusion | flops 262144 | bytes 3145792 | tf_op jit(solution)/shard_map/while/body/scatter-add | solution.py:24
  124.4 3.4 %scatter_fusion = f32[128,128,128]{2,0,1:T(8,128)} fusion(f32[128,128,128]{2,0,1:T(8,128)} %get-tuple-element.361, s32[16]{0:T(128)S(1)} %compare_select_fusion.8, f32[16,128,128]{2,1,0:T(8,128)S(1)} %copy.56), kind=kCustom, calls=%fused_computation.2.clone.1 | custom fusion | flops 262144 | bytes 3145792 | tf_op jit(solution)/shard_map/while/body/scatter-add | solution.py:24
  133.4 3.3 %scatter_fusion = f32[128,128,128]{2,0,1:T(8,128)} fusion(f32[128,128,128]{2,0,1:T(8,128)} %get-tuple-element.361, s32[16]{0:T(128)S(1)} %compare_select_fusion.8, f32[16,128,128]{2,1,0:T(8,128)S(1)} %copy.56), kind=kCustom, calls=%fused_computation.2.clone.1 | custom fusion | flops 262144 | bytes 3145792 | tf_op jit(solution)/shard_map/while/body/scatter-add | solution.py:24
  136.7 3.1 %copy.47 = bf16[128,4,2048]{0,2,1:T(8,128)(2,1)S(1)} copy(bf16[128,4,2048]{2,0,1:T(8,128)(2,1)} %all-gather.4.cloned.1.call-done) | data formatting | bytes 4194304 | tf_op jit(solution)/shard_map/all_gather | solution.py:48
  139.8 3.0 %copy.49 = bf16[128,64,128]{2,0,1:T(8,128)(2,1)} copy(bf16[128,64,128]{0,2,1:T(8,128)(2,1)S(1)} %bitcast.48) | data formatting | bytes 4194304 | tf_op jit(solution)/shard_map/while | solution.py:26
  142.8 13.4 %while.24 = (s32[]{:T(128)}, f32[128,128,128]{2,0,1:T(8,128)}, s32[32]{0:T(128)S(1)}, bf16[32,128,128]{2,1,0:T(8,128)(2,1)S(1)}, s32[32]{0:T(128)S(1)}, /*index=...) while((s32[]{:T(128)}, f32[128,128,128]{2,0,1:T(8,128)}, s32[32]{0:T(128)S(1)}, ...), condition=%wide.region_5.6_spmd, body=%wide.region_3.5_spmd.sunk | while | flops 67896520 | bytes 8394419 | solution.py:26
  146.1 3.4 %scatter_fusion.1 = f32[128,128,128]{2,0,1:T(8,128)} fusion(f32[128,128,128]{2,0,1:T(8,128)} %get-tuple-element.395, s32[16]{0:T(128)S(1)} %compare_select_fusion.9, f32[16,128,128]{2,1,0:T(8,128)S(1)} %copy.57), kind=kCustom, calls=%fused_computation.3.clone.1 | custom fusion | flops 262144 | bytes 3145792 | tf_op jit(solution)/shard_map/while/body/eval_jaxpr/scatter-add | solution.py:24
  152.8 3.4 %scatter_fusion.1 = f32[128,128,128]{2,0,1:T(8,128)} fusion(f32[128,128,128]{2,0,1:T(8,128)} %get-tuple-element.395, s32[16]{0:T(128)S(1)} %compare_select_fusion.9, f32[16,128,128]{2,1,0:T(8,128)S(1)} %copy.57), kind=kCustom, calls=%fused_computation.3.clone.1 | custom fusion | flops 262144 | bytes 3145792 | tf_op jit(solution)/shard_map/while/body/eval_jaxpr/scatter-add | solution.py:24
  156.2 6.3 %convert_element_type.46 = bf16[128,128,128]{2,0,1:T(8,128)(2,1)} convert(f32[128,128,128]{2,0,1:T(8,128)} %get-tuple-element.158) | non-fusion elementwise | flops 2097152 | bytes 12582912 | tf_op jit(solution)/shard_map/convert_element_type | solution.py:74
  162.6 6.4 %copy.50 = bf16[128,128,128]{0,2,1:T(8,128)(2,1)} copy(bf16[128,128,128]{2,0,1:T(8,128)(2,1)} %convert_element_type.46) | data formatting | bytes 8388608 | tf_op jit(solution)/shard_map/convert_element_type | solution.py:74
  170.9 111.8 %reduce-scatter.2.cloned.1.call-done = bf16[128,1,4096]{0,2,1:T(8,128)(2,1)} async-done(((bf16[128,1,16384]{0,2,1:T(8,128)(2,1)}), bf16[128,1,4096]{0,2,1:T(8,128)(2,1)}) %reduce-scatter.2.cloned.1.call-update) | async-done | bytes 1048592 | tf_op jit(solution)/shard_map/reduce_scatter | solution.py:73
  (115 shorter events, 83.9 us)
Async XLA Ops:
  6.5 276.2 %copy-start = (bf16[128,256]{1,0:T(8,128)(2,1)S(1)}, bf16[128,256]{1,0:T(8,128)(2,1)}, u32[]{:S(2)}) copy-start(bf16[128,256]{1,0:T(8,128)(2,1)} %param.17) | copy-start | bytes 196612
  6.5 130.2 %all-gather.4.cloned.1.call-start = ((), (), s32[]{:S(2)}) async-start(), calls=%async_computation.1 | async-start | bytes 2621440 | tf_op jit(solution)/shard_map/all_gather | solution.py:48
  8.5 162.4 %all-gather.6.cloned.1.call-start = ((), (), s32[]{:S(2)}) async-start(), calls=%async_computation.3 | async-start | bytes 3145728 | tf_op jit(solution)/shard_map/all_gather | solution.py:81
  10.9 271.8 %reduce-scatter.2.cloned.1.call-start = ((), (), s32[]{:S(2)}) async-start(), calls=%async_computation.2 | async-start | bytes 5242880 | tf_op jit(solution)/shard_map/reduce_scatter | solution.py:73
  24.6 4.3 %copy-start.4 = (s32[256,1]{0,1:T(1,128)S(1)}, s32[256,1]{0,1:T(1,128)}, u32[]{:S(2)}) copy-start(s32[256,1]{0,1:T(1,128)} %param.20) | copy-start | bytes 3076
  24.6 4.3 %copy-start.6 = (s32[256,1]{0,1:T(1,128)S(1)}, s32[256,1]{0,1:T(1,128)}, u32[]{:S(2)}) copy-start(s32[256,1]{0,1:T(1,128)} %param.21) | copy-start | bytes 3076
  136.7 6.1 %copy-start.1 = (bf16[32,128,128]{2,1,0:T(8,128)(2,1)S(1)}, bf16[32,128,128]{2,1,0:T(8,128)(2,1)}, u32[]{:S(2)}) copy-start(bf16[32,128,128]{2,1,0:T(8,128)(2,1)} %param.23) | copy-start | bytes 3145732
  136.7 6.1 %copy-start.3 = (s32[32,1]{0,1:T(1,128)S(1)}, s32[32,1]{0,1:T(1,128)}, u32[]{:S(2)}) copy-start(s32[32,1]{0,1:T(1,128)} %param.24) | copy-start | bytes 388
  136.7 6.1 %copy-start.7 = (s32[32,1]{0,1:T(1,128)S(1)}, s32[32,1]{0,1:T(1,128)}, u32[]{:S(2)}) copy-start(s32[32,1]{0,1:T(1,128)} %param.25) | copy-start | bytes 388
  168.9 1.2 copy-start.2
  168.9 113.7 %copy-start.5 = (s32[1,4096]{1,0:T(1,128)S(1)}, s32[1,4096]{1,0:T(1,128)}, u32[]{:S(2)}) copy-start(s32[1,4096]{1,0:T(1,128)} %param.27) | copy-start | bytes 49156
  168.9 113.7 %copy-start.8 = (s32[128]{0:T(128)S(1)}, s32[128]{0:T(128)}, u32[]{:S(2)}) copy-start(s32[128]{0:T(128)} %param.26) | copy-start | bytes 1540
Sparse Core Ops, SparseCore 0:
  8.9 24.0 all-gather.3
  34.6 32.6 all-gather.5
  169.1 113.5 reduce-scatter.1
where the time goes:
time: 298 us; the launch traced here: 293 us
  waiting for transfers between devices  112 us (38%)
  local copies, waits for them, and re-layouts  80.3 us (27%)
  other arithmetic  63.8 us (21%)
  matrix products  23 us (8%)
  between operations  13.8 us (5%)
    reduce_scatter x1, waiting for transfers between devices, per_device(): lax.psum_scatter(partial_sum.astype(jnp.bfloat16), 'sec', scatter_dimensi...  112 us
    scatter-add x14, other arithmetic, one_turn(): return running.at[:, group_targets].add(contribution)  47.4 us
    gather x14, local copies, waits for them, and re-layouts, one_turn(): picked = jnp.take(source_blocks, group_sources, axis=1)  38.5 us
    dot_general x14, matrix products, one_turn(): jnp.einsum('rtk,tkc->rtc', picked, group_tiles, preferred_element_type=jn...  20.3 us
    while x2, local copies, waits for them, and re-layouts, apply_tiles(): return lax.fori_loop(0, turn_count, one_turn, totals)  9.55 us
    and x14, other arithmetic, one_turn(): picked = jnp.take(source_blocks, group_sources, axis=1)  8.86 us
    unnamed x20, local copies, waits for them, and re-layouts  8.29 us
    convert_element_type x1, local copies, waits for them, and re-layouts, per_device(): partial_sum.astype(jnp.bfloat16)  6.37 us
  transfers between devices with their start and end apart: 3, of which 1 were waited for; matrix products, arithmetic and copies ran while one was open for 55% of the time, Pallas kernels for 0%

commit v1 on v0

v1 whole, which is shorter than its diff:
```python
import functools

import jax
import jax.numpy as jnp
from jax import lax
from jax.experimental import pallas as pl
from jax.experimental.pallas import tpu as pltpu
from jax.sharding import PartitionSpec as P

TILE = 128
PANEL = 2048
GROUP = 32
UNROLL = 8
PIECES = 2
VMEM = 48 * 1024 * 1024


def ladder_kernel(sources, targets, live, amps, tiles, out, acc):
    step = pl.program_id(0)
    blocks_per_chunk = out.shape[2] // TILE

    @pl.when(step == 0)
    def _():
        @pl.loop(0, acc.shape[0])
        def _(b):
            acc[b] = jnp.zeros(acc.shape[1:], jnp.float32)

    here = jnp.clip(live[0] - step * tiles.shape[0], 0, tiles.shape[0])

    def product(t):
        s = pl.multiple_of(sources[step * tiles.shape[0] + t] * TILE, TILE)
        return jnp.dot(amps[:, pl.ds(s, TILE)], tiles[t], preferred_element_type=jnp.float32)

    def add(t, value):
        b = targets[step * tiles.shape[0] + t]
        acc[b] = acc[b] + value

    full = here // UNROLL

    @pl.loop(0, full)
    def _(g):
        values = [product(g * UNROLL + u) for u in range(UNROLL)]
        for u in range(UNROLL):
            add(g * UNROLL + u, values[u])

    @pl.loop(full * UNROLL, here)
    def _(t):
        add(t, product(t))

    @pl.when(step == pl.num_programs(0) - 1)
    def _():
        for c in range(out.shape[0]):

            @pl.loop(0, blocks_per_chunk)
            def _(b):
                columns = pl.ds(pl.multiple_of(b * TILE, TILE), TILE)
                out[c, :, columns] = acc[c * blocks_per_chunk + b].astype(out.dtype)


def ladder_term(amps, tiles, sources, targets, live, chunk_count):
    rows, width = amps.shape
    count = tiles.shape[0]
    group = GROUP if count % GROUP == 0 else count
    chunk = width // chunk_count
    return pl.pallas_call(
        ladder_kernel,
        grid_spec=pltpu.PrefetchScalarGridSpec(
            num_scalar_prefetch=3,
            grid=(count // group,),
            in_specs=[
                pl.BlockSpec((rows, width), lambda g, s, t, n: (0, 0)),
                pl.BlockSpec(
                    (group, TILE, TILE),
                    lambda g, s, t, n: (jnp.minimum(g, jnp.maximum(n[0] - 1, 0) // group), 0, 0),
                ),
            ],
            out_specs=pl.BlockSpec((chunk_count, rows, chunk), lambda g, s, t, n: (0, 0, 0)),
            scratch_shapes=[pltpu.VMEM((width // TILE, rows, TILE), jnp.float32)],
        ),
        out_shape=jax.ShapeDtypeStruct((chunk_count, rows, chunk), jnp.bfloat16),
        compiler_params=pltpu.CompilerParams(vmem_limit_bytes=VMEM),
        cost_estimate=pl.CostEstimate(
            flops=8 * count * rows * TILE * TILE, bytes_accessed=40 * 1024 * 1024, transcendentals=0
        ),
        name="ladder",
    )(sources, targets, live, amps, tiles)


def cycle_kernel(slots, blocks, targets, chunks, ladder, tiles, *rest):
    pieces, out, panel, acc, sems = rest[:-4], rest[-4], rest[-3], rest[-2], rest[-1]
    step = pl.program_id(0)
    blocks_per_chunk = acc.shape[0]
    first = chunks[step] * blocks_per_chunk
    copies = [pltpu.make_async_copy(p, panel.at[j], sems.at[j]) for j, p in enumerate(pieces)]

    @pl.when(step == 0)
    def _():
        for copy in copies:
            copy.start()

    @pl.loop(0, blocks_per_chunk)
    def _(b):
        columns = pl.ds(pl.multiple_of(b * TILE, TILE), TILE)
        acc[b] = ladder[0, :, columns].astype(jnp.float32)

    @pl.when(step == 0)
    def _():
        for copy in copies:
            copy.wait()

    @pl.loop(0, tiles.shape[0])
    def _(t):
        b = targets[t] - first

        @pl.when((b >= 0) & (b < blocks_per_chunk))
        def _():
            columns = pl.ds(pl.multiple_of(blocks[t] * TILE, TILE), TILE)
            acc[b] = acc[b] + jnp.dot(
                panel[slots[t], :, columns], tiles[t], preferred_element_type=jnp.float32
            )

    @pl.loop(0, blocks_per_chunk)
    def _(b):
        columns = pl.ds(pl.multiple_of(b * TILE, TILE), TILE)
        out[0, :, columns] = acc[b].astype(out.dtype)


def add_cycle(ladder, tiles, pieces, slots, blocks, targets, chunks):
    _, rows, chunk = ladder.shape
    count = chunks.shape[0]
    return pl.pallas_call(
        cycle_kernel,
        grid_spec=pltpu.PrefetchScalarGridSpec(
            num_scalar_prefetch=4,
            grid=(count,),
            in_specs=[
                pl.BlockSpec((1, rows, chunk), lambda i, s, b, t, c: (c[i], 0, 0)),
                pl.BlockSpec(tiles.shape, lambda i, s, b, t, c: (0, 0, 0)),
            ]
            + [pl.BlockSpec(memory_space=pl.ANY)] * len(pieces),
            out_specs=pl.BlockSpec((1, rows, chunk), lambda i, s, b, t, c: (i, 0, 0)),
            scratch_shapes=[
                pltpu.VMEM((len(pieces),) + pieces[0].shape, jnp.bfloat16),
                pltpu.VMEM((chunk // TILE, rows, TILE), jnp.float32),
                pltpu.SemaphoreType.DMA((len(pieces),)),
            ],
        ),
        out_shape=jax.ShapeDtypeStruct((count, rows, chunk), jnp.bfloat16),
        compiler_params=pltpu.CompilerParams(vmem_limit_bytes=VMEM),
        cost_estimate=pl.CostEstimate(
            flops=2 * tiles.shape[0] * rows * TILE * TILE,
            bytes_accessed=8 * 1024 * 1024,
            transcendentals=0,
        ),
        name="cycle",
    )(slots, blocks, targets, chunks, ladder, tiles, *pieces)


def per_device(
    sec_count,
    inner_count,
    amplitudes,
    hole_ladder,
    bare_integrals,
    ladder_tiles,
    ladder_source,
    ladder_target,
    ladder_live,
    cycle_tiles,
    cycle_source,
    cycle_target,
    gap_rows,
    gap_columns,
):
    rows, _, width = amplitudes.shape
    owned = bare_integrals.shape[2]
    n = sec_count
    z = lax.axis_index("sec")
    me = lax.axis_index("inner")
    amps = amplitudes.reshape(rows, width)

    held = {0: amps[:, :PANEL]}
    bit = inner_count // 2
    while bit:
        pairs = [(i, i ^ bit) for i in range(inner_count)]
        for j in list(held):
            held[j ^ bit] = lax.ppermute(held[j], "inner", pairs)
        bit //= 2
    pieces = [held[j] for j in range(inner_count)]
    panel_blocks = PANEL // TILE
    source = cycle_source[:, 0]
    slots = jnp.bitwise_xor(source // panel_blocks, me)
    blocks = source % panel_blocks
    targets = cycle_target[:, 0]

    ladder = ladder_term(
        amps, ladder_tiles, ladder_source[:, 0], ladder_target[:, 0], ladder_live[:, 0], n
    )
    finish = functools.partial(add_cycle, ladder, cycle_tiles, pieces, slots, blocks, targets)
    edge = jnp.where(z == 0, n - 1, 0).astype(jnp.int32)
    first_share = finish(edge[None])[0]
    shares = finish(jnp.arange(n, dtype=jnp.int32))

    cut = rows // PIECES
    parts = [slice(p * cut, (p + 1) * cut) for p in range(PIECES)]

    def share(index, p):
        picked = lax.dynamic_slice(shares, (jnp.clip(index, 0, n - 1), p * cut, 0), (1, cut, owned))
        return picked[0]

    def plus(a, b):
        return (a.astype(jnp.float32) + b.astype(jnp.float32)).astype(jnp.bfloat16)

    going_up, going_down = [None] * PIECES, [None] * PIECES
    for t in range(1, n):
        up_pairs = [(i, i + 1) for i in range(t)]
        down_pairs = [(n - 1 - i, n - 2 - i) for i in range(t)]
        for p in range(PIECES):
            if t == 1:
                up = down = first_share[parts[p]]
            else:
                up = plus(share(n - t + z, p), going_up[p])
                down = plus(share(t - n + z, p), going_down[p])
            going_up[p] = lax.ppermute(up, "sec", up_pairs)
            going_down[p] = lax.ppermute(down, "sec", down_pairs)

    owned_amps = lax.dynamic_slice(amps, (0, z * owned), (rows, owned))
    hole = jnp.dot(
        hole_ladder,
        lax.all_gather(owned_amps, "row", axis=0, tiled=True),
        preferred_element_type=jnp.float32,
    )
    own = lax.dynamic_index_in_dim(shares, z, 0, keepdims=False)
    base = bare_integrals[:, 0, :].astype(jnp.float32) + hole + own.astype(jnp.float32)
    joined = [
        going_up[p].astype(jnp.float32) + going_down[p].astype(jnp.float32) for p in range(PIECES)
    ]
    residual = base + jnp.concatenate(joined, axis=0)
    denominator = (gap_rows[:, None] + gap_columns[0][None, :]).astype(jnp.float32) / 1024.0
    updated = (residual / denominator).astype(jnp.bfloat16)
    return updated.reshape(rows, 1, owned)


def solution(mesh):
    in_specs = (
        P("row", "inner", None),
        P("row", None),
        P("row", "inner", "sec"),
        P("sec", "inner", None),
        P("sec", "inner"),
        P("sec", "inner"),
        P("sec", "inner"),
        P("sec", "inner", None),
        P("sec", "inner"),
        P("sec", "inner"),
        P("row"),
        P("inner", "sec"),
    )
    return jax.shard_map(
        functools.partial(per_device, mesh.shape["sec"], mesh.shape["inner"]),
        mesh=mesh,
        in_specs=in_specs,
        out_specs=P("row", "inner", "sec"),
        check_vma=False,
    )
```

time: 298 us -> 165 us (0.55)
  local copies, waits for them, and re-layouts: 80.3 us -> 7.94 us
  other arithmetic: 63.8 us -> 8.73 us
  waiting for transfers between devices: 112 us -> 68.6 us
  starting transfers between devices: 0.09 us -> 36 us
  Pallas kernels: 0 us -> 23.2 us
  matrix products: 23 us -> 4.15 us
    reduce_scatter x1 -> x0, waiting for transfers between devices: 112 us -> none  [per_device(): lax.psum_scatter(partial_sum.astype(jnp.bfloat16), 'sec', scatter_dimensi...]
    ppermute x0 -> x15, waiting for transfers between devices: none -> 55.8 us  [the longest x6 28.6 us: per_device(): going_down[p] = lax.ppermute(down, 'sec', down_pairs)]
    scatter-add x14 -> x0, other arithmetic: 47.4 us -> none  [one_turn(): return running.at[:, group_targets].add(contribution)]
    gather x14 -> x0, local copies, waits for them, and re-layouts: 38.5 us -> none  [one_turn(): picked = jnp.take(source_blocks, group_sources, axis=1)]
    ppermute x0 -> x15, starting transfers between devices: none -> 36 us  [the longest x6 21.4 us: per_device(): going_down[p] = lax.ppermute(down, 'sec', down_pairs)]
    pallas_call x0 -> x3, Pallas kernels: none -> 23.2 us  [the longest x2 14.3 us: add_cycle(): pl.pallas_call(cycle_kernel, grid_spec=pltpu.PrefetchScalarGridSpec(num_s...]
    dot_general x14 -> x0, matrix products: 20.3 us -> none  [one_turn(): jnp.einsum('rtk,tkc->rtc', picked, group_tiles, preferred_element_type=jn...]
    all_gather x1, waiting for transfers between devices: 0.02 us -> 12.7 us  [per_device(): lax.all_gather(owned_amps, 'row', axis=0, tiled=True)]
  transfers between devices with their start and end apart: 3 -> 16, of which waited for: 1 -> 10; matrix products, arithmetic and copies ran while one was open for 55% -> 5% of each run, Pallas kernels for 0% -> 12%
where the time goes in v1:
time: 165 us; the launch traced here: 163 us
  waiting for transfers between devices  68.6 us (42%)
  starting transfers between devices  36 us (22%)
  Pallas kernels  23.2 us (14%)
  between operations  14.3 us (9%)
  other arithmetic  8.73 us (5%)
  local copies, waits for them, and re-layouts  7.94 us (5%)
  matrix products  4.15 us (3%)
    ppermute x6, waiting for transfers between devices, per_device(): going_down[p] = lax.ppermute(down, 'sec', down_pairs)  28.6 us
    ppermute x6, starting transfers between devices, per_device(): going_down[p] = lax.ppermute(down, 'sec', down_pairs)  21.4 us
    ppermute x6, waiting for transfers between devices, per_device(): going_up[p] = lax.ppermute(up, 'sec', up_pairs)  17.2 us
    pallas_call x2, Pallas kernels, add_cycle(): pl.pallas_call(cycle_kernel, grid_spec=pltpu.PrefetchScalarGridSpec(num_s...  14.3 us
    all_gather x1, waiting for transfers between devices, per_device(): lax.all_gather(owned_amps, 'row', axis=0, tiled=True)  12.7 us
    ppermute x6, starting transfers between devices, per_device(): going_up[p] = lax.ppermute(up, 'sec', up_pairs)  10.8 us
    ppermute x3, waiting for transfers between devices, per_device(): held[j ^ bit] = lax.ppermute(held[j], 'inner', pairs)  9.95 us
    pallas_call x1, Pallas kernels, ladder_term(): pl.pallas_call(ladder_kernel, grid_spec=pltpu.PrefetchScalarGridSpec(num_...  8.89 us
  transfers between devices with their start and end apart: 16, of which 10 were waited for; matrix products, arithmetic and copies ran while one was open for 5% of the time, Pallas kernels for 12%

profile of v1, /device:TPU:17, one launch (start us, length us, event | category | flops | bytes accessed | tf_op | source)
XLA Modules:
  0.0 162.8 jit_solution(13506414892337393565)
XLA Ops:
  10.6 9.9 %collective-permute-done.1.rest_2_ = bf16[128,2048]{1,0:T(8,128)(2,1)S(1)} collective-permute-done((bf16[128,2048]{1,0:T(8,128)(2,1)S(1)}, bf16[128,2048]{1,0:T(8,128)(2,1)S(1)}, u32[]{:S(2)}, u32[]{:S(2)}) %collective-permute-start.1) | collective-permute-done | bytes 524320 | tf_op jit(solution)/shard_map/ppermute | solution.py:187
  20.5 1.5 collective-permute-start.2
  24.1 8.9 %ladder.1 = bf16[4,128,4096]{2,1,0:T(8,128)(2,1)S(1)} custom-call(s32[256]{0:T(256)S(1)} %bitcast.79, s32[256]{0:T(256)S(1)} %bitcast.80, s32[1]{0:T(128)} %bitcast.76.live, bf16[128,16384]{1,0:T(8,128)(2,1)} %bitcast.82, bf16[256,128,128]{2,1,0:T(8,128)(2,1)} %tiles.3), custom_call_target="tpu_custom_call" | custom-call | flops 4294967296 | bytes 41943040 | tf_op jit(solution)/shard_map/ladder/pallas_call | solution.py:65
  33.0 2.0 %copy-done.1 = bf16[4,128,4096]{2,1,0:T(8,128)(2,1)} copy-done((bf16[4,128,4096]{2,1,0:T(8,128)(2,1)}, bf16[4,128,4096]{2,1,0:T(8,128)(2,1)S(1)}, u32[]{:S(2)}) %copy-start.1) | copy-done | bytes 4194328
  35.0 3.9 %cycle.3 = bf16[1,128,4096]{2,1,0:T(8,128)(2,1)S(1)} custom-call(s32[32]{0:T(128)S(1)} %get-tuple-element.15.slots, s32[32]{0:T(128)S(1)} %get-tuple-element.14.blocks, s32[32]{0:T(128)S(1)} %bitcast.77, s32[1]{0:T(128)} %bitcast.12.chunks, bf16[4,128,4096]{2,1,0:T(8,128)(2,1)} %copy-done.1, bf16[32,128,128]{2,1,0:T(8,128)(2,1)S(1)} %copy-done.2, ...), custom_call_target="tpu_custom_call" | custom-call | flops 134217728 | bytes 8388608 | tf_op jit(solution)/shard_map/cycle/pallas_call | solution.py:131
  45.6 10.4 %cycle.2 = bf16[4,128,4096]{2,1,0:T(8,128)(2,1)} custom-call(s32[32]{0:T(128)S(1)} %get-tuple-element.15.slots, s32[32]{0:T(128)S(1)} %get-tuple-element.14.blocks, s32[32]{0:T(128)S(1)} %bitcast.78, s32[4]{0:T(128)S(1)} %iota.3.chunks, bf16[4,128,4096]{2,1,0:T(8,128)(2,1)} %copy-done.1, bf16[32,128,128]{2,1,0:T(8,128)(2,1)S(1)} %copy-done.2, ...), custom_call_target="tpu_custom_call" | custom-call | flops 134217728 | bytes 8388608 | tf_op jit(solution)/shard_map/cycle/pallas_call | solution.py:131
  58.6 8.3 %collective-permute-done.12 = bf16[64,4096]{1,0:T(8,128)(2,1)} collective-permute-done((bf16[64,4096]{1,0:T(8,128)(2,1)}, bf16[64,4096]{1,0:T(8,128)(2,1)}, u32[]{:S(2)}, u32[]{:S(2)}) %collective-permute-start.12) | collective-permute-done | bytes 524320 | tf_op jit(solution)/shard_map/ppermute | solution.py:225
  67.0 6.9 %collective-permute-done.4 = bf16[64,4096]{1,0:T(8,128)(2,1)S(1)} collective-permute-done((bf16[64,4096]{1,0:T(8,128)(2,1)S(1)}, bf16[64,4096]{1,0:T(8,128)(2,1)S(1)}, u32[]{:S(2)}, u32[]{:S(2)}) %collective-permute-start.4) | collective-permute-done | bytes 524320 | tf_op jit(solution)/shard_map/ppermute | solution.py:224
  73.9 3.6 %fusion.11 = (bf16[64,4096]{1,0:T(8,128)(2,1)}, bf16[64,4096]{1,0:T(8,128)(2,1)S(1)}, bf16[64,4096]{1,0:T(8,128)(2,1)S(1)}, bf16[64,4096]{1,0:T(8,128)(2,1)S(1)}) fusion(bf16[64,4096]{1,0:T(8,128)(2,1)S(1)} %collective-permute-done.4, bf16[4,128,4096]{2,1,0:T(8,128)(2,1)} %cycle.2, s32[]{:T(128)S(6)} %min.17, bf16[64,4096]{1,0:T(8,128)(2,1)} %collective-permute-done.12, ...), kind=kLoop, calls=%fused_computation.22 | loop fusion | flops 4194304 | bytes 6291468 | tf_op jit(solution)/shard_map/convert_element_type | solution.py:212
  78.7 9.5 %collective-permute-start.13 = (bf16[64,4096]{1,0:T(8,128)(2,1)S(1)}, bf16[64,4096]{1,0:T(8,128)(2,1)S(1)}, u32[]{:S(2)}, u32[]{:S(2)}) collective-permute-start(bf16[64,4096]{1,0:T(8,128)(2,1)S(1)} %get-tuple-element.6), channel_id=1, source_target_pairs={{24,16},{16,8},{25,17},{17,9},{26,18},{18,10},{27,19},{19,11},{28,... | collective-permute-start | bytes 1572872 | tf_op jit(solution)/shard_map/ppermute | solution.py:225
  88.2 1.9 %collective-permute-start.7 = (bf16[64,4096]{1,0:T(8,128)(2,1)S(1)}, bf16[64,4096]{1,0:T(8,128)(2,1)S(1)}, u32[]{:S(2)}, u32[]{:S(2)}) collective-permute-start(bf16[64,4096]{1,0:T(8,128)(2,1)S(1)} %get-tuple-element.8), channel_id=1, source_target_pairs={{24,16},{16,8},{25,17},{17,9},{26,18},{18,10},{27,19},{19,11},{28,... | collective-permute-start | bytes 1572872 | tf_op jit(solution)/shard_map/ppermute | solution.py:225
  90.1 3.4 %collective-permute-start.5 = (bf16[64,4096]{1,0:T(8,128)(2,1)}, bf16[64,4096]{1,0:T(8,128)(2,1)}, u32[]{:S(2)}, u32[]{:S(2)}) collective-permute-start(bf16[64,4096]{1,0:T(8,128)(2,1)} %get-tuple-element.5), channel_id=1, source_target_pairs={{0,8},{8,16},{16,24},{1,9},{9,17},{17,25},{2,10},{10,18},{18,26},{... | collective-permute-start | bytes 1572872 | tf_op jit(solution)/shard_map/ppermute | solution.py:224
  93.5 5.3 %collective-permute-done.10 = bf16[64,4096]{1,0:T(8,128)(2,1)S(1)} collective-permute-done((bf16[64,4096]{1,0:T(8,128)(2,1)S(1)}, bf16[64,4096]{1,0:T(8,128)(2,1)S(1)}, u32[]{:S(2)}, u32[]{:S(2)}) %collective-permute-start.10) | collective-permute-done | bytes 524320 | tf_op jit(solution)/shard_map/ppermute | solution.py:224
  99.7 11.2 %collective-permute-done.7 = bf16[64,4096]{1,0:T(8,128)(2,1)S(1)} collective-permute-done((bf16[64,4096]{1,0:T(8,128)(2,1)S(1)}, bf16[64,4096]{1,0:T(8,128)(2,1)S(1)}, u32[]{:S(2)}, u32[]{:S(2)}) %collective-permute-start.7) | collective-permute-done | bytes 524320 | tf_op jit(solution)/shard_map/ppermute | solution.py:225
  111.0 1.9 %fusion.9 = (bf16[64,4096]{1,0:T(8,128)(2,1)S(1)}, bf16[64,4096]{1,0:T(8,128)(2,1)S(1)}, bf16[64,4096]{1,0:T(8,128)(2,1)S(1)}) fusion(bf16[64,4096]{1,0:T(8,128)(2,1)S(1)} %collective-permute-done.7, bf16[4,128,4096]{2,1,0:T(8,128)(2,1)} %cycle.2, s32[]{:T(128)S(6)} %min.19, bf16[64,4096]{1,0:T(8,128)(2,1)S(1)} %collective-permute-done.13, ...), kind=kLoop, calls=%fused_computation.18 | loop fusion | flops 3145728 | bytes 4718600 | tf_op jit(solution)/shard_map/convert_element_type | solution.py:212
  112.8 4.1 %collective-permute-start.8 = (bf16[64,4096]{1,0:T(8,128)(2,1)S(1)}, bf16[64,4096]{1,0:T(8,128)(2,1)S(1)}, u32[]{:S(2)}, u32[]{:S(2)}) collective-permute-start(bf16[64,4096]{1,0:T(8,128)(2,1)S(1)} %get-tuple-element.9), channel_id=1, source_target_pairs={{24,16},{16,8},{8,0},{25,17},{17,9},{9,1},{26,18},{18,10},{10,2},{... | collective-permute-start | bytes 1572872 | tf_op jit(solution)/shard_map/ppermute | solution.py:225
  117.0 2.3 %constant_dynamic-slice_fusion = bf16[128,1,4096]{2,0,1:T(8,128)(2,1)} fusion(bf16[128,1,16384]{2,0,1:T(8,128)(2,1)} %param.12, s32[]{:T(128)S(6)} %select_n.31), kind=kLoop, calls=%fused_computation.28 | loop fusion | bytes 2097156 | tf_op jit(solution)/shard_map/dynamic_slice | solution.py:227
  119.3 1.9 %collective-permute-start.11 = (bf16[64,4096]{1,0:T(8,128)(2,1)S(1)}, bf16[64,4096]{1,0:T(8,128)(2,1)S(1)}, u32[]{:S(2)}, u32[]{:S(2)}) collective-permute-start(bf16[64,4096]{1,0:T(8,128)(2,1)S(1)} %get-tuple-element.11), channel_id=1, source_target_pairs={{0,8},{8,16},{16,24},{1,9},{9,17},{17,25},{2,10},{10,18},{18,26},{... | collective-permute-start | bytes 1572872 | tf_op jit(solution)/shard_map/ppermute | solution.py:224
  121.2 3.4 %collective-permute-start.14 = (bf16[64,4096]{1,0:T(8,128)(2,1)S(1)}, bf16[64,4096]{1,0:T(8,128)(2,1)S(1)}, u32[]{:S(2)}, u32[]{:S(2)}) collective-permute-start(bf16[64,4096]{1,0:T(8,128)(2,1)S(1)} %get-tuple-element.10), channel_id=1, source_target_pairs={{24,16},{16,8},{8,0},{25,17},{17,9},{9,1},{26,18},{18,10},{10,2},{... | collective-permute-start | bytes 1572872 | tf_op jit(solution)/shard_map/ppermute | solution.py:225
  124.6 3.0 %collective-permute-done.8 = bf16[64,4096]{1,0:T(8,128)(2,1)S(1)} collective-permute-done((bf16[64,4096]{1,0:T(8,128)(2,1)S(1)}, bf16[64,4096]{1,0:T(8,128)(2,1)S(1)}, u32[]{:S(2)}, u32[]{:S(2)}) %collective-permute-start.8) | collective-permute-done | bytes 524320 | tf_op jit(solution)/shard_map/ppermute | solution.py:225
  128.8 5.0 %collective-permute-done.11 = bf16[64,4096]{1,0:T(8,128)(2,1)S(1)} collective-permute-done((bf16[64,4096]{1,0:T(8,128)(2,1)S(1)}, bf16[64,4096]{1,0:T(8,128)(2,1)S(1)}, u32[]{:S(2)}, u32[]{:S(2)}) %collective-permute-start.11) | collective-permute-done | bytes 524320 | tf_op jit(solution)/shard_map/ppermute | solution.py:224
  133.9 5.1 %collective-permute-done.14 = bf16[64,4096]{1,0:T(8,128)(2,1)S(1)} collective-permute-done((bf16[64,4096]{1,0:T(8,128)(2,1)S(1)}, bf16[64,4096]{1,0:T(8,128)(2,1)S(1)}, u32[]{:S(2)}, u32[]{:S(2)}) %collective-permute-start.14) | collective-permute-done | bytes 524320 | tf_op jit(solution)/shard_map/ppermute | solution.py:225
  139.1 12.7 %all-gather.3.cloned.1.call-done = bf16[256,1,4096]{2,0,1:T(8,128)(2,1)} async-done(((bf16[128,1,4096]{2,0,1:T(8,128)(2,1)}), bf16[256,1,4096]{2,0,1:T(8,128)(2,1)}) %all-gather.3.cloned.1.call-update) | async-done | bytes 2097168 | tf_op jit(solution)/shard_map/all_gather | solution.py:230
  151.8 4.1 %fusion.12 = bf16[128,1,4096]{2,0,1:T(8,128)(2,1)} fusion(s32[4096]{0:T(1024)S(1)} %bitcast.83, s32[128]{0:T(128)S(1)} %copy-done.7, f32[64,4096]{1,0:T(8,128)S(1)} %convert_add_fusion.9, f32[64,4096]{1,0:T(8,128)S(1)} %convert_add_fusion.10, bf16[4,128,4096]{2,1,0:T(8,128)(2,1)} %cycle.2, s32[]{:T(128)S(6)} %select_n.34, bf16[128,256]{1,0:T(8,128)(2,1)S(1)} %copy-done, ...), kind=kOutput, calls=%fused_computation.25 | convolution fusion | flops 274202624 | bytes 7422468 | tf_op jit(solution)/shard_map/dot_general | solution.py:228
  (39 shorter events, 18.2 us)
Async XLA Ops:
  6.5 145.3 %copy-start = (bf16[128,256]{1,0:T(8,128)(2,1)S(1)}, bf16[128,256]{1,0:T(8,128)(2,1)}, u32[]{:S(2)}) copy-start(bf16[128,256]{1,0:T(8,128)(2,1)} %param.13) | copy-start | bytes 196612
  6.5 145.3 %all-gather.3.cloned.1.call-start = ((), (), s32[]{:S(2)}) async-start(), calls=%async_computation | async-start | bytes 3145728 | tf_op jit(solution)/shard_map/all_gather | solution.py:230
  7.7 12.9 %collective-permute-start.1 = (bf16[128,2048]{1,0:T(8,128)(2,1)S(1)}, bf16[128,2048]{1,0:T(8,128)(2,1)S(1)}, u32[]{:S(2)}, u32[]{:S(2)}) collective-permute-start(bf16[128,2048]{1,0:T(8,128)(2,1)S(1)} %slice.20.rest_0_), channel_id=1, source_target_pairs={{0,2},{1,3},{2,0},{3,1},{4,6},{5,7},{6,4},{7,5},{8,10},{9,11},{10,... | collective-permute-start | bytes 1572872 | tf_op jit(solution)/shard_map/ppermute | solution.py:187
  9.0 26.1 %collective-permute-start = (bf16[128,2048]{1,0:T(8,128)(2,1)S(1)}, bf16[128,2048]{1,0:T(8,128)(2,1)S(1)}, u32[]{:S(2)}, u32[]{:S(2)}) collective-permute-start(bf16[128,2048]{1,0:T(8,128)(2,1)S(1)} %slice.20.rest_0_), channel_id=1, source_target_pairs={{0,1},{1,0},{2,3},{3,2},{4,5},{5,4},{6,7},{7,6},{8,9},{9,8},{10,11... | collective-permute-start | bytes 1572872 | tf_op jit(solution)/shard_map/ppermute | solution.py:187
  20.5 14.5 %collective-permute-start.2 = (bf16[128,2048]{1,0:T(8,128)(2,1)S(1)}, bf16[128,2048]{1,0:T(8,128)(2,1)S(1)}, u32[]{:S(2)}, u32[]{:S(2)}) collective-permute-start(bf16[128,2048]{1,0:T(8,128)(2,1)S(1)} %collective-permute-done.1.rest_2_), channel_id=1, source_target_pairs={{0,1},{1,0},{2,3},{3,2},{4,5},{5,4},{6,7},{7,6},{8,9},{9,8},{10,11... | collective-permute-start | bytes 1572872 | tf_op jit(solution)/shard_map/ppermute | solution.py:187
  22.7 0.7 copy-start.4
  23.4 0.7 copy-start.5
  24.1 10.9 %copy-start.2 = (bf16[32,128,128]{2,1,0:T(8,128)(2,1)S(1)}, bf16[32,128,128]{2,1,0:T(8,128)(2,1)}, u32[]{:S(2)}) copy-start(bf16[32,128,128]{2,1,0:T(8,128)(2,1)} %tiles.5) | copy-start | bytes 3145732
  24.1 10.9 %copy-start.3 = (s32[32,1]{0,1:T(1,128)S(1)}, s32[32,1]{0,1:T(1,128)}, u32[]{:S(2)}) copy-start(s32[32,1]{0,1:T(1,128)} %param.21) | copy-start | bytes 388
  33.0 2.0 %copy-start.1 = (bf16[4,128,4096]{2,1,0:T(8,128)(2,1)}, bf16[4,128,4096]{2,1,0:T(8,128)(2,1)S(1)}, u32[]{:S(2)}) copy-start(bf16[4,128,4096]{2,1,0:T(8,128)(2,1)S(1)} %ladder.1) | copy-start | bytes 12582916
  40.0 15.9 %collective-permute-start.3 = (bf16[64,4096]{1,0:T(8,128)(2,1)}, bf16[64,4096]{1,0:T(8,128)(2,1)}, u32[]{:S(2)}, u32[]{:S(2)}) collective-permute-start(bf16[64,4096]{1,0:T(8,128)(2,1)} %get-tuple-element.12), channel_id=1, source_target_pairs={{0,8},{1,9},{2,10},{3,11},{4,12},{5,13},{6,14},{7,15}} | collective-permute-start | bytes 1572872 | tf_op jit(solution)/shard_map/ppermute | solution.py:224
  41.5 25.5 %collective-permute-start.6 = (bf16[64,4096]{1,0:T(8,128)(2,1)}, bf16[64,4096]{1,0:T(8,128)(2,1)}, u32[]{:S(2)}, u32[]{:S(2)}) collective-permute-start(bf16[64,4096]{1,0:T(8,128)(2,1)} %get-tuple-element.12), channel_id=1, source_target_pairs={{24,16},{25,17},{26,18},{27,19},{28,20},{29,21},{30,22},{31,23}} | collective-permute-start | bytes 1572872 | tf_op jit(solution)/shard_map/ppermute | solution.py:225
  42.8 24.2 %collective-permute-start.12 = (bf16[64,4096]{1,0:T(8,128)(2,1)}, bf16[64,4096]{1,0:T(8,128)(2,1)}, u32[]{:S(2)}, u32[]{:S(2)}) collective-permute-start(bf16[64,4096]{1,0:T(8,128)(2,1)} %get-tuple-element.13), channel_id=1, source_target_pairs={{24,16},{25,17},{26,18},{27,19},{28,20},{29,21},{30,22},{31,23}} | collective-permute-start | bytes 1572872 | tf_op jit(solution)/shard_map/ppermute | solution.py:225
  44.1 22.9 %collective-permute-start.9 = (bf16[64,4096]{1,0:T(8,128)(2,1)}, bf16[64,4096]{1,0:T(8,128)(2,1)}, u32[]{:S(2)}, u32[]{:S(2)}) collective-permute-start(bf16[64,4096]{1,0:T(8,128)(2,1)} %get-tuple-element.13), channel_id=1, source_target_pairs={{0,8},{1,9},{2,10},{3,11},{4,12},{5,13},{6,14},{7,15}} | collective-permute-start | bytes 1572872 | tf_op jit(solution)/shard_map/ppermute | solution.py:224
  57.3 16.5 %collective-permute-start.4 = (bf16[64,4096]{1,0:T(8,128)(2,1)S(1)}, bf16[64,4096]{1,0:T(8,128)(2,1)S(1)}, u32[]{:S(2)}, u32[]{:S(2)}) collective-permute-start(bf16[64,4096]{1,0:T(8,128)(2,1)S(1)} %fusion.10), channel_id=1, source_target_pairs={{0,8},{8,16},{1,9},{9,17},{2,10},{10,18},{3,11},{11,19},{4,12},{12... | collective-permute-start | bytes 1572872 | tf_op jit(solution)/shard_map/ppermute | solution.py:224
  77.4 21.4 %collective-permute-start.10 = (bf16[64,4096]{1,0:T(8,128)(2,1)S(1)}, bf16[64,4096]{1,0:T(8,128)(2,1)S(1)}, u32[]{:S(2)}, u32[]{:S(2)}) collective-permute-start(bf16[64,4096]{1,0:T(8,128)(2,1)S(1)} %get-tuple-element.7), channel_id=1, source_target_pairs={{0,8},{8,16},{1,9},{9,17},{2,10},{10,18},{3,11},{11,19},{4,12},{12... | collective-permute-start | bytes 1572872 | tf_op jit(solution)/shard_map/ppermute | solution.py:224
  78.7 21.0 %collective-permute-start.13 = (bf16[64,4096]{1,0:T(8,128)(2,1)S(1)}, bf16[64,4096]{1,0:T(8,128)(2,1)S(1)}, u32[]{:S(2)}, u32[]{:S(2)}) collective-permute-start(bf16[64,4096]{1,0:T(8,128)(2,1)S(1)} %get-tuple-element.6), channel_id=1, source_target_pairs={{24,16},{16,8},{25,17},{17,9},{26,18},{18,10},{27,19},{19,11},{28,... | collective-permute-start | bytes 1572872 | tf_op jit(solution)/shard_map/ppermute | solution.py:225
  88.2 22.8 %collective-permute-start.7 = (bf16[64,4096]{1,0:T(8,128)(2,1)S(1)}, bf16[64,4096]{1,0:T(8,128)(2,1)S(1)}, u32[]{:S(2)}, u32[]{:S(2)}) collective-permute-start(bf16[64,4096]{1,0:T(8,128)(2,1)S(1)} %get-tuple-element.8), channel_id=1, source_target_pairs={{24,16},{16,8},{25,17},{17,9},{26,18},{18,10},{27,19},{19,11},{28,... | collective-permute-start | bytes 1572872 | tf_op jit(solution)/shard_map/ppermute | solution.py:225
  90.1 34.5 %collective-permute-start.5 = (bf16[64,4096]{1,0:T(8,128)(2,1)}, bf16[64,4096]{1,0:T(8,128)(2,1)}, u32[]{:S(2)}, u32[]{:S(2)}) collective-permute-start(bf16[64,4096]{1,0:T(8,128)(2,1)} %get-tuple-element.5), channel_id=1, source_target_pairs={{0,8},{8,16},{16,24},{1,9},{9,17},{17,25},{2,10},{10,18},{18,26},{... | collective-permute-start | bytes 1572872 | tf_op jit(solution)/shard_map/ppermute | solution.py:224
  112.8 14.8 %collective-permute-start.8 = (bf16[64,4096]{1,0:T(8,128)(2,1)S(1)}, bf16[64,4096]{1,0:T(8,128)(2,1)S(1)}, u32[]{:S(2)}, u32[]{:S(2)}) collective-permute-start(bf16[64,4096]{1,0:T(8,128)(2,1)S(1)} %get-tuple-element.9), channel_id=1, source_target_pairs={{24,16},{16,8},{8,0},{25,17},{17,9},{9,1},{26,18},{18,10},{10,2},{... | collective-permute-start | bytes 1572872 | tf_op jit(solution)/shard_map/ppermute | solution.py:225
  119.3 14.6 %collective-permute-start.11 = (bf16[64,4096]{1,0:T(8,128)(2,1)S(1)}, bf16[64,4096]{1,0:T(8,128)(2,1)S(1)}, u32[]{:S(2)}, u32[]{:S(2)}) collective-permute-start(bf16[64,4096]{1,0:T(8,128)(2,1)S(1)} %get-tuple-element.11), channel_id=1, source_target_pairs={{0,8},{8,16},{16,24},{1,9},{9,17},{17,25},{2,10},{10,18},{18,26},{... | collective-permute-start | bytes 1572872 | tf_op jit(solution)/shard_map/ppermute | solution.py:224
  121.2 30.6 %copy-start.6 = (s32[1,4096]{1,0:T(1,128)S(1)}, s32[1,4096]{1,0:T(1,128)}, u32[]{:S(2)}) copy-start(s32[1,4096]{1,0:T(1,128)} %param.23) | copy-start | bytes 49156
  121.2 30.6 %copy-start.7 = (s32[128]{0:T(128)S(1)}, s32[128]{0:T(128)}, u32[]{:S(2)}) copy-start(s32[128]{0:T(128)} %param.22) | copy-start | bytes 1540
  121.2 17.8 %collective-permute-start.14 = (bf16[64,4096]{1,0:T(8,128)(2,1)S(1)}, bf16[64,4096]{1,0:T(8,128)(2,1)S(1)}, u32[]{:S(2)}, u32[]{:S(2)}) collective-permute-start(bf16[64,4096]{1,0:T(8,128)(2,1)S(1)} %get-tuple-element.10), channel_id=1, source_target_pairs={{24,16},{16,8},{8,0},{25,17},{17,9},{9,1},{26,18},{18,10},{10,2},{... | collective-permute-start | bytes 1572872 | tf_op jit(solution)/shard_map/ppermute | solution.py:225
Sparse Core Ops, SparseCore 0:
  119.4 32.3 all-gather.2

commit v2 on v1

--- a/solution.py
+++ b/solution.py
@@ -12,7 +12,7 @@
 GROUP = 32
 UNROLL = 8
 PIECES = 2
-VMEM = 48 * 1024 * 1024
+VMEM = 60 * 1024 * 1024
 
 
 def ladder_kernel(sources, targets, live, amps, tiles, out, acc):
@@ -87,7 +87,9 @@
 
 
 def cycle_kernel(slots, blocks, targets, chunks, ladder, tiles, *rest):
-    pieces, out, panel, acc, sems = rest[:-4], rest[-4], rest[-3], rest[-2], rest[-1]
+    panel, acc, sems = rest[-3:]
+    outs = rest[-3 - PIECES : -3]
+    pieces = rest[: -3 - PIECES]
     step = pl.program_id(0)
     blocks_per_chunk = acc.shape[0]
     first = chunks[step] * blocks_per_chunk
@@ -122,7 +124,10 @@
     @pl.loop(0, blocks_per_chunk)
     def _(b):
         columns = pl.ds(pl.multiple_of(b * TILE, TILE), TILE)
-        out[0, :, columns] = acc[b].astype(out.dtype)
+        value = acc[b].astype(outs[0].dtype)
+        cut = outs[0].shape[1]
+        for p in range(PIECES):
+            outs[p][0, :, columns] = value[p * cut : (p + 1) * cut]
 
 
 def add_cycle(ladder, tiles, pieces, slots, blocks, targets, chunks):
@@ -138,14 +143,15 @@
                 pl.BlockSpec(tiles.shape, lambda i, s, b, t, c: (0, 0, 0)),
             ]
             + [pl.BlockSpec(memory_space=pl.ANY)] * len(pieces),
-            out_specs=pl.BlockSpec((1, rows, chunk), lambda i, s, b, t, c: (i, 0, 0)),
+            out_specs=[pl.BlockSpec((1, rows // PIECES, chunk), lambda i, s, b, t, c: (i, 0, 0))]
+            * PIECES,
             scratch_shapes=[
                 pltpu.VMEM((len(pieces),) + pieces[0].shape, jnp.bfloat16),
                 pltpu.VMEM((chunk // TILE, rows, TILE), jnp.float32),
                 pltpu.SemaphoreType.DMA((len(pieces),)),
             ],
         ),
-        out_shape=jax.ShapeDtypeStruct((count, rows, chunk), jnp.bfloat16),
+        out_shape=[jax.ShapeDtypeStruct((count, rows // PIECES, chunk), jnp.bfloat16)] * PIECES,
         compiler_params=pltpu.CompilerParams(vmem_limit_bytes=VMEM),
         cost_estimate=pl.CostEstimate(
             flops=2 * tiles.shape[0] * rows * TILE * TILE,
@@ -179,12 +185,21 @@
     me = lax.axis_index("inner")
     amps = amplitudes.reshape(rows, width)
 
+    owned_amps = lax.dynamic_slice(amps, (0, z * owned), (rows, owned))
+    owned_all = lax.all_gather(owned_amps, "row", axis=0, tiled=True)
+
+    ladder = ladder_term(
+        amps, ladder_tiles, ladder_source[:, 0], ladder_target[:, 0], ladder_live[:, 0], n
+    )
+
     held = {0: amps[:, :PANEL]}
     bit = inner_count // 2
     while bit:
         pairs = [(i, i ^ bit) for i in range(inner_count)]
         for j in list(held):
             held[j ^ bit] = lax.ppermute(held[j], "inner", pairs)
+        if bit == inner_count // 2 and bit > 1:
+            held[bit], ladder = lax.optimization_barrier((held[bit], ladder))
         bit //= 2
     pieces = [held[j] for j in range(inner_count)]
     panel_blocks = PANEL // TILE
@@ -193,47 +208,49 @@
     blocks = source % panel_blocks
     targets = cycle_target[:, 0]
 
-    ladder = ladder_term(
-        amps, ladder_tiles, ladder_source[:, 0], ladder_target[:, 0], ladder_live[:, 0], n
-    )
     finish = functools.partial(add_cycle, ladder, cycle_tiles, pieces, slots, blocks, targets)
     edge = jnp.where(z == 0, n - 1, 0).astype(jnp.int32)
-    first_share = finish(edge[None])[0]
+    first_shares = finish(edge[None])
     shares = finish(jnp.arange(n, dtype=jnp.int32))
 
-    cut = rows // PIECES
-    parts = [slice(p * cut, (p + 1) * cut) for p in range(PIECES)]
+    hole = jnp.dot(hole_ladder, owned_all, preferred_element_type=jnp.float32)
+    base = bare_integrals[:, 0, :].astype(jnp.float32) + hole
 
     def share(index, p):
-        picked = lax.dynamic_slice(shares, (jnp.clip(index, 0, n - 1), p * cut, 0), (1, cut, owned))
-        return picked[0]
+        return lax.dynamic_index_in_dim(shares[p], jnp.clip(index, 0, n - 1), 0, keepdims=False)
 
     def plus(a, b):
         return (a.astype(jnp.float32) + b.astype(jnp.float32)).astype(jnp.bfloat16)
 
-    going_up, going_down = [None] * PIECES, [None] * PIECES
+    going = [None] * PIECES
     for t in range(1, n):
         up_pairs = [(i, i + 1) for i in range(t)]
         down_pairs = [(n - 1 - i, n - 2 - i) for i in range(t)]
         for p in range(PIECES):
             if t == 1:
-                up = down = first_share[parts[p]]
+                up = down = first_shares[p][0]
+            elif 2 * t <= n:
+                up = down = share(jnp.where(z < t, n - t + z, t - n + z), p)
+                if len(going[p]) == 1:
+                    up = down = plus(up, going[p][0])
+                else:
+                    up = down = plus(up, jnp.where(z < t, going[p][0], going[p][1]))
             else:
-                up = plus(share(n - t + z, p), going_up[p])
-                down = plus(share(t - n + z, p), going_down[p])
-            going_up[p] = lax.ppermute(up, "sec", up_pairs)
-            going_down[p] = lax.ppermute(down, "sec", down_pairs)
-
-    owned_amps = lax.dynamic_slice(amps, (0, z * owned), (rows, owned))
-    hole = jnp.dot(
-        hole_ladder,
-        lax.all_gather(owned_amps, "row", axis=0, tiled=True),
-        preferred_element_type=jnp.float32,
-    )
-    own = lax.dynamic_index_in_dim(shares, z, 0, keepdims=False)
-    base = bare_integrals[:, 0, :].astype(jnp.float32) + hole + own.astype(jnp.float32)
+                up = plus(share(n - t + z, p), going[p][0])
+                down = plus(share(t - n + z, p), going[p][-1])
+            if 2 * t < n - 1:
+                going[p] = [lax.ppermute(up, "sec", up_pairs + down_pairs)]
+            else:
+                going[p] = [
+                    lax.ppermute(up, "sec", up_pairs),
+                    lax.ppermute(down, "sec", down_pairs),
+                ]
+            if t == 1 and p == PIECES - 1:
+                going[0][0], base = lax.optimization_barrier((going[0][0], base))
+
     joined = [
-        going_up[p].astype(jnp.float32) + going_down[p].astype(jnp.float32) for p in range(PIECES)
+        share(z, p).astype(jnp.float32) + sum(g.astype(jnp.float32) for g in going[p])
+        for p in range(PIECES)
     ]
     residual = base + jnp.concatenate(joined, axis=0)
     denominator = (gap_rows[:, None] + gap_columns[0][None, :]).astype(jnp.float32) / 1024.0

time: 165 us -> 119 us (0.72)
  waiting for transfers between devices: 68.6 us -> 29.4 us
  Pallas kernels: 23.2 us -> 34 us
  starting transfers between devices: 36 us -> 26.2 us
  local copies, waits for them, and re-layouts: 7.94 us -> 4.75 us
  matrix products: 4.15 us -> 2.19 us
    ppermute x12 -> x10, waiting for transfers between devices: 45.9 us -> 28.1 us  [the longest x4 25.7 us: per_device(): lax.ppermute(down, 'sec', down_pairs)]
    all_gather x1, waiting for transfers between devices: 12.7 us -> 0.02 us  [per_device(): owned_all = lax.all_gather(owned_amps, 'row', axis=0, tiled=True)]
    ppermute x3, waiting for transfers between devices: 9.95 us -> 1.2 us  [per_device(): held[j ^ bit] = lax.ppermute(held[j], 'inner', pairs)]
    ppermute x12 -> x10, starting transfers between devices: 32.2 us -> 23.9 us  [the longest x4 11.8 us: per_device(): lax.ppermute(down, 'sec', down_pairs)]
    pallas_call x1, Pallas kernels: 8.89 us -> 16 us  [ladder_term(): pl.pallas_call(ladder_kernel, grid_spec=pltpu.PrefetchScalarGridSpec(num_...]
    pallas_call x2, Pallas kernels: 14.3 us -> 18 us  [add_cycle(): pl.pallas_call(cycle_kernel, grid_spec=pltpu.PrefetchScalarGridSpec(num_s...]
    unnamed x16 -> x22, local copies, waits for them, and re-layouts: 3.4 us -> 0.84 us
    dot_general x1, matrix products: 4.15 us -> 2.19 us  [per_device(): hole = jnp.dot(hole_ladder, owned_all, preferred_element_type=jnp.float32)]
  transfers between devices with their start and end apart: 16 -> 14, of which waited for: 10 -> 7; matrix products, arithmetic and copies ran while one was open for 5% -> 9% of each run, Pallas kernels for 12% -> 29%
where the time goes in v2:
time: 119 us; the launch traced here: 118 us
  Pallas kernels  34 us (29%)
  waiting for transfers between devices  29.4 us (25%)
  starting transfers between devices  26.2 us (22%)
  between operations  14.3 us (12%)
  other arithmetic  7.37 us (6%)
  local copies, waits for them, and re-layouts  4.75 us (4%)
  matrix products  2.19 us (2%)
    ppermute x4, waiting for transfers between devices, per_device(): lax.ppermute(down, 'sec', down_pairs)  25.7 us
    pallas_call x2, Pallas kernels, add_cycle(): pl.pallas_call(cycle_kernel, grid_spec=pltpu.PrefetchScalarGridSpec(num_s...  18 us
    pallas_call x1, Pallas kernels, ladder_term(): pl.pallas_call(ladder_kernel, grid_spec=pltpu.PrefetchScalarGridSpec(num_...  16 us
    ppermute x4, starting transfers between devices, per_device(): lax.ppermute(down, 'sec', down_pairs)  11.8 us
    ppermute x4, starting transfers between devices, per_device(): lax.ppermute(up, 'sec', up_pairs)  9.48 us
    convert_element_type x4, other arithmetic, plus(): return (a.astype(jnp.float32) + b.astype(jnp.float32)).astype(jnp.bfloat16)  4.86 us
    ppermute x2, starting transfers between devices, per_device(): going[p] = [lax.ppermute(up, 'sec', up_pairs + down_pairs)]  2.58 us
  transfers between devices with their start and end apart: 14, of which 7 were waited for; matrix products, arithmetic and copies ran while one was open for 9% of the time, Pallas kernels for 29%

profile of v2, /device:TPU:17, one launch (start us, length us, event | category | flops | bytes accessed | tf_op | source)
XLA Modules:
  0.0 118.2 jit_solution(15019168103394998694)
XLA Ops:
  7.7 1.3 %collective-permute-start = (bf16[128,2048]{1,0:T(8,128)(2,1)S(1)}, bf16[128,2048]{1,0:T(8,128)(2,1)S(1)}, u32[]{:S(2)}, u32[]{:S(2)}) collective-permute-start(bf16[128,2048]{1,0:T(8,128)(2,1)S(1)} %slice.4.rest_0_), channel_id=1, source_target_pairs={{0,2},{1,3},{2,0},{3,1},{4,6},{5,7},{6,4},{7,5},{8,10},{9,11},{10,... | collective-permute-start | bytes 1572872 | tf_op jit(solution)/shard_map/ppermute | solution.py:200
  9.9 2.3 %constant_dynamic-slice_fusion = bf16[128,1,4096]{2,0,1:T(8,128)(2,1)} fusion(bf16[128,1,16384]{2,0,1:T(8,128)(2,1)} %param.12, s32[]{:T(128)S(6)} %select_n.35), kind=kLoop, calls=%fused_computation.21 | loop fusion | bytes 2097156 | tf_op jit(solution)/shard_map/dynamic_slice | solution.py:188
  12.9 16.0 %ladder.1 = bf16[4,128,4096]{2,1,0:T(8,128)(2,1)} custom-call(s32[256]{0:T(256)} %bitcast.69, s32[256]{0:T(256)} %bitcast.70, s32[1]{0:T(128)} %bitcast.63.live, bf16[128,16384]{1,0:T(8,128)(2,1)} %bitcast.65, bf16[256,128,128]{2,1,0:T(8,128)(2,1)} %tiles.3), custom_call_target="tpu_custom_call" | custom-call | flops 4294967296 | bytes 41943040 | tf_op jit(solution)/shard_map/ladder/pallas_call | solution.py:65
  31.6 6.1 %cycle.2 = (bf16[1,64,4096]{2,1,0:T(8,128)(2,1)}, bf16[1,64,4096]{2,1,0:T(8,128)(2,1)}) custom-call(s32[32]{0:T(128)} %get-tuple-element.26.slots, s32[32]{0:T(128)} %get-tuple-element.25.blocks, s32[32]{0:T(128)} %bitcast.67, s32[1]{0:T(128)} %bitcast.2.chunks, bf16[4,128,4096]{2,1,0:T(8,128)(2,1)} %ladder.1, bf16[32,128,128]{2,1,0:T(8,128)(2,1)} %tiles.5, ...), custom_call_target="tpu_custom_call" | custom-call | flops 134217728 | bytes 8388608 | tf_op jit(solution)/shard_map/cycle/pallas_call | solution.py:136
  37.7 1.3 %collective-permute-start.8 = (bf16[64,4096]{1,0:T(8,128)(2,1)}, bf16[64,4096]{1,0:T(8,128)(2,1)S(1)}, u32[]{:S(2)}, u32[]{:S(2)}) collective-permute-start(bf16[64,4096]{1,0:T(8,128)(2,1)} %bitcast.72), channel_id=1, source_target_pairs={{0,8},{24,16},{1,9},{25,17},{2,10},{26,18},{3,11},{27,19},{4,12},{... | collective-permute-start | bytes 1572872 | tf_op jit(solution)/shard_map/ppermute | solution.py:242
  39.1 1.3 %collective-permute-start.3 = (bf16[64,4096]{1,0:T(8,128)(2,1)}, bf16[64,4096]{1,0:T(8,128)(2,1)}, u32[]{:S(2)}, u32[]{:S(2)}) collective-permute-start(bf16[64,4096]{1,0:T(8,128)(2,1)} %bitcast.71), channel_id=1, source_target_pairs={{0,8},{24,16},{1,9},{25,17},{2,10},{26,18},{3,11},{27,19},{4,12},{... | collective-permute-start | bytes 1572872 | tf_op jit(solution)/shard_map/ppermute | solution.py:242
  40.9 11.9 %cycle.3 = (bf16[4,64,4096]{2,1,0:T(8,128)(2,1)}, bf16[4,64,4096]{2,1,0:T(8,128)(2,1)}) custom-call(s32[32]{0:T(128)} %get-tuple-element.26.slots, s32[32]{0:T(128)} %get-tuple-element.25.blocks, s32[32]{0:T(128)} %bitcast.68, s32[4]{0:T(128)} %iota.3.chunks, bf16[4,128,4096]{2,1,0:T(8,128)(2,1)} %ladder.1, bf16[32,128,128]{2,1,0:T(8,128)(2,1)} %tiles.5, ...), custom_call_target="tpu_custom_call" | custom-call | flops 134217728 | bytes 8388608 | tf_op jit(solution)/shard_map/cycle/pallas_call | solution.py:136
  53.5 2.0 %fusion.5 = bf16[64,4096]{1,0:T(8,128)(2,1)} fusion(bf16[64,4096]{1,0:T(8,128)(2,1)S(1)} %collective-permute-done.8, bf16[4,64,4096]{2,1,0:T(8,128)(2,1)} %get-tuple-element.19, s32[]{:T(128)S(6)} %min.19), kind=kLoop, calls=%fused_computation.9 | loop fusion | flops 1048576 | bytes 1572868 | tf_op jit(solution)/shard_map/convert_element_type | solution.py:223
  55.5 1.4 %collective-permute-start.9 = (bf16[64,4096]{1,0:T(8,128)(2,1)}, bf16[64,4096]{1,0:T(8,128)(2,1)}, u32[]{:S(2)}, u32[]{:S(2)}) collective-permute-start(bf16[64,4096]{1,0:T(8,128)(2,1)} %fusion.5), channel_id=1, source_target_pairs={{0,8},{8,16},{1,9},{9,17},{2,10},{10,18},{3,11},{11,19},{4,12},{12... | collective-permute-start | bytes 1572872 | tf_op jit(solution)/shard_map/ppermute | solution.py:245
  56.9 4.0 %collective-permute-start.11 = (bf16[64,4096]{1,0:T(8,128)(2,1)}, bf16[64,4096]{1,0:T(8,128)(2,1)}, u32[]{:S(2)}, u32[]{:S(2)}) collective-permute-start(bf16[64,4096]{1,0:T(8,128)(2,1)} %fusion.5), channel_id=1, source_target_pairs={{24,16},{16,8},{25,17},{17,9},{26,18},{18,10},{27,19},{19,11},{28,... | collective-permute-start | bytes 1572872 | tf_op jit(solution)/shard_map/ppermute | solution.py:246
  61.0 2.2 %fusion = f32[128,4096]{1,0:T(8,128)S(1)} fusion(bf16[128,256]{1,0:T(8,128)(2,1)S(1)} %copy-done, bf16[256,1,4096]{2,0,1:T(8,128)(2,1)} %all-gather.3.cloned.1.call-done, bf16[128,1,4096]{2,0,1:T(8,128)(2,1)S(1)} %copy-done.7), kind=kOutput, calls=%fused_computation.1 | convolution fusion | flops 269484032 | bytes 5308416 | tf_op jit(solution)/shard_map/dot_general | solution.py:216
  63.2 1.7 %collective-permute-done.3 = bf16[64,4096]{1,0:T(8,128)(2,1)} collective-permute-done((bf16[64,4096]{1,0:T(8,128)(2,1)}, bf16[64,4096]{1,0:T(8,128)(2,1)}, u32[]{:S(2)}, u32[]{:S(2)}) %collective-permute-start.3) | collective-permute-done | bytes 524320 | tf_op jit(solution)/shard_map/ppermute | solution.py:242
  66.0 1.3 %collective-permute-start.4 = (bf16[64,4096]{1,0:T(8,128)(2,1)S(1)}, bf16[64,4096]{1,0:T(8,128)(2,1)S(1)}, u32[]{:S(2)}, u32[]{:S(2)}) collective-permute-start(bf16[64,4096]{1,0:T(8,128)(2,1)S(1)} %fusion.8), channel_id=1, source_target_pairs={{0,8},{8,16},{1,9},{9,17},{2,10},{10,18},{3,11},{11,19},{4,12},{12... | collective-permute-start | bytes 1572872 | tf_op jit(solution)/shard_map/ppermute | solution.py:245
  67.3 4.0 %collective-permute-start.6 = (bf16[64,4096]{1,0:T(8,128)(2,1)S(1)}, bf16[64,4096]{1,0:T(8,128)(2,1)S(1)}, u32[]{:S(2)}, u32[]{:S(2)}) collective-permute-start(bf16[64,4096]{1,0:T(8,128)(2,1)S(1)} %fusion.8), channel_id=1, source_target_pairs={{24,16},{16,8},{25,17},{17,9},{26,18},{18,10},{27,19},{19,11},{28,... | collective-permute-start | bytes 1572872 | tf_op jit(solution)/shard_map/ppermute | solution.py:246
  71.3 4.8 %collective-permute-done.11 = bf16[64,4096]{1,0:T(8,128)(2,1)} collective-permute-done((bf16[64,4096]{1,0:T(8,128)(2,1)}, bf16[64,4096]{1,0:T(8,128)(2,1)}, u32[]{:S(2)}, u32[]{:S(2)}) %collective-permute-start.11) | collective-permute-done | bytes 524320 | tf_op jit(solution)/shard_map/ppermute | solution.py:246
  76.1 1.5 %fusion.6 = (bf16[64,4096]{1,0:T(8,128)(2,1)S(1)}, bf16[64,4096]{1,0:T(8,128)(2,1)S(1)}) fusion(bf16[64,4096]{1,0:T(8,128)(2,1)} %collective-permute-done.9, bf16[4,64,4096]{2,1,0:T(8,128)(2,1)S(1)} %copy-done.3, s32[]{:T(128)S(6)} %min.18, bf16[64,4096]{1,0:T(8,128)(2,1)} %collective-permute-done.11, s32[]{:T(128)S(6)} %min.20), kind=kLoop, calls=%fused_computation.11 | loop fusion | flops 2097152 | bytes 3145736 | tf_op jit(solution)/shard_map/convert_element_type | solution.py:223
  77.6 1.9 %collective-permute-start.12 = (bf16[64,4096]{1,0:T(8,128)(2,1)S(1)}, bf16[64,4096]{1,0:T(8,128)(2,1)S(1)}, u32[]{:S(2)}, u32[]{:S(2)}) collective-permute-start(bf16[64,4096]{1,0:T(8,128)(2,1)S(1)} %get-tuple-element.24), channel_id=1, source_target_pairs={{24,16},{16,8},{8,0},{25,17},{17,9},{9,1},{26,18},{18,10},{10,2},{... | collective-permute-start | bytes 1572872 | tf_op jit(solution)/shard_map/ppermute | solution.py:246
  79.5 3.4 %collective-permute-start.10 = (bf16[64,4096]{1,0:T(8,128)(2,1)S(1)}, bf16[64,4096]{1,0:T(8,128)(2,1)S(1)}, u32[]{:S(2)}, u32[]{:S(2)}) collective-permute-start(bf16[64,4096]{1,0:T(8,128)(2,1)S(1)} %get-tuple-element.23), channel_id=1, source_target_pairs={{0,8},{8,16},{16,24},{1,9},{9,17},{17,25},{2,10},{10,18},{18,26},{... | collective-permute-start | bytes 1572872 | tf_op jit(solution)/shard_map/ppermute | solution.py:245
  82.9 4.3 %collective-permute-done.6 = bf16[64,4096]{1,0:T(8,128)(2,1)S(1)} collective-permute-done((bf16[64,4096]{1,0:T(8,128)(2,1)S(1)}, bf16[64,4096]{1,0:T(8,128)(2,1)S(1)}, u32[]{:S(2)}, u32[]{:S(2)}) %collective-permute-start.6) | collective-permute-done | bytes 524320 | tf_op jit(solution)/shard_map/ppermute | solution.py:246
  87.5 1.9 %collective-permute-start.7 = (bf16[64,4096]{1,0:T(8,128)(2,1)S(1)}, bf16[64,4096]{1,0:T(8,128)(2,1)S(1)}, u32[]{:S(2)}, u32[]{:S(2)}) collective-permute-start(bf16[64,4096]{1,0:T(8,128)(2,1)S(1)} %get-tuple-element.22), channel_id=1, source_target_pairs={{24,16},{16,8},{8,0},{25,17},{17,9},{9,1},{26,18},{18,10},{10,2},{... | collective-permute-start | bytes 1572872 | tf_op jit(solution)/shard_map/ppermute | solution.py:246
  89.4 3.4 %collective-permute-start.5 = (bf16[64,4096]{1,0:T(8,128)(2,1)S(1)}, bf16[64,4096]{1,0:T(8,128)(2,1)S(1)}, u32[]{:S(2)}, u32[]{:S(2)}) collective-permute-start(bf16[64,4096]{1,0:T(8,128)(2,1)S(1)} %get-tuple-element.21), channel_id=1, source_target_pairs={{0,8},{8,16},{16,24},{1,9},{9,17},{17,25},{2,10},{10,18},{18,26},{... | collective-permute-start | bytes 1572872 | tf_op jit(solution)/shard_map/ppermute | solution.py:245
  92.8 5.6 %collective-permute-done.12 = bf16[64,4096]{1,0:T(8,128)(2,1)S(1)} collective-permute-done((bf16[64,4096]{1,0:T(8,128)(2,1)S(1)}, bf16[64,4096]{1,0:T(8,128)(2,1)S(1)}, u32[]{:S(2)}, u32[]{:S(2)}) %collective-permute-start.12) | collective-permute-done | bytes 524320 | tf_op jit(solution)/shard_map/ppermute | solution.py:246
  98.6 11.1 %collective-permute-done.7 = bf16[64,4096]{1,0:T(8,128)(2,1)S(1)} collective-permute-done((bf16[64,4096]{1,0:T(8,128)(2,1)S(1)}, bf16[64,4096]{1,0:T(8,128)(2,1)S(1)}, u32[]{:S(2)}, u32[]{:S(2)}) %collective-permute-start.7) | collective-permute-done | bytes 524320 | tf_op jit(solution)/shard_map/ppermute | solution.py:246
  109.9 1.5 %fusion.10 = bf16[128,1,4096]{2,0,1:T(8,128)(2,1)} fusion(s32[4096]{0:T(1024)S(1)} %bitcast.66, s32[128]{0:T(128)S(1)} %copy-done.10, f32[128,4096]{1,0:T(8,128)S(1)} %fusion, f32[64,4096]{1,0:T(8,128)S(1)} %convert_add_fusion.3, f32[64,4096]{1,0:T(8,128)S(1)} %convert_add_fusion.7), kind=kLoop, calls=%fused_computation.20 | loop fusion | flops 3670016 | bytes 5259776 | tf_op jit(solution)/shard_map/reshape | solution.py:258
  (42 shorter events, 7.9 us)
Async XLA Ops:
  6.5 54.4 %copy-start = (bf16[128,256]{1,0:T(8,128)(2,1)S(1)}, bf16[128,256]{1,0:T(8,128)(2,1)}, u32[]{:S(2)}) copy-start(bf16[128,256]{1,0:T(8,128)(2,1)} %param.13) | copy-start | bytes 196612
  6.5 54.4 %all-gather.3.cloned.1.call-start = ((), (), s32[]{:S(2)}) async-start(), calls=%async_computation | async-start | bytes 3145728 | tf_op jit(solution)/shard_map/all_gather | solution.py:189
  7.7 21.2 %copy-start.1 = (bf16[128,2048]{1,0:T(8,128)(2,1)}, bf16[128,2048]{1,0:T(8,128)(2,1)S(1)}, u32[]{:S(2)}) copy-start(bf16[128,2048]{1,0:T(8,128)(2,1)S(1)} %slice.4.rest_0_) | copy-start | bytes 1572868
  7.7 21.2 %collective-permute-start = (bf16[128,2048]{1,0:T(8,128)(2,1)S(1)}, bf16[128,2048]{1,0:T(8,128)(2,1)S(1)}, u32[]{:S(2)}, u32[]{:S(2)}) collective-permute-start(bf16[128,2048]{1,0:T(8,128)(2,1)S(1)} %slice.4.rest_0_), channel_id=1, source_target_pairs={{0,2},{1,3},{2,0},{3,1},{4,6},{5,7},{6,4},{7,5},{8,10},{9,11},{10,... | collective-permute-start | bytes 1572872 | tf_op jit(solution)/shard_map/ppermute | solution.py:200
  9.0 20.7 %collective-permute-start.1 = (bf16[128,2048]{1,0:T(8,128)(2,1)S(1)}, bf16[128,2048]{1,0:T(8,128)(2,1)S(1)}, u32[]{:S(2)}, u32[]{:S(2)}) collective-permute-start(bf16[128,2048]{1,0:T(8,128)(2,1)S(1)} %slice.4.rest_0_), channel_id=1, source_target_pairs={{0,1},{1,0},{2,3},{3,2},{4,5},{5,4},{6,7},{7,6},{8,9},{9,8},{10,11... | collective-permute-start | bytes 1572872 | tf_op jit(solution)/shard_map/ppermute | solution.py:200
  12.9 16.1 %copy-start.9 = (s32[32,1]{0,1:T(1,128)S(1)}, s32[32,1]{0,1:T(1,128)}, u32[]{:S(2)}) copy-start(s32[32,1]{0,1:T(1,128)} %param.20) | copy-start | bytes 388
  28.9 2.0 %copy-start.4 = (bf16[128,2048]{1,0:T(8,128)(2,1)}, bf16[128,2048]{1,0:T(8,128)(2,1)S(1)}, u32[]{:S(2)}) copy-start(bf16[128,2048]{1,0:T(8,128)(2,1)S(1)} %collective-permute-done.rest_2_) | copy-start | bytes 1572868
  28.9 2.0 %collective-permute-start.2 = (bf16[128,2048]{1,0:T(8,128)(2,1)S(1)}, bf16[128,2048]{1,0:T(8,128)(2,1)S(1)}, u32[]{:S(2)}, u32[]{:S(2)}) collective-permute-start(bf16[128,2048]{1,0:T(8,128)(2,1)S(1)} %collective-permute-done.rest_2_), channel_id=1, source_target_pairs={{0,1},{1,0},{2,3},{3,2},{4,5},{5,4},{6,7},{7,6},{8,9},{9,8},{10,11... | collective-permute-start | bytes 1572872 | tf_op jit(solution)/shard_map/ppermute | solution.py:200
  29.7 1.2 %copy-start.5 = (bf16[128,2048]{1,0:T(8,128)(2,1)}, bf16[128,2048]{1,0:T(8,128)(2,1)S(1)}, u32[]{:S(2)}) copy-start(bf16[128,2048]{1,0:T(8,128)(2,1)S(1)} %collective-permute-done.1.rest_1_) | copy-start | bytes 1572868
  37.7 15.8 %collective-permute-start.8 = (bf16[64,4096]{1,0:T(8,128)(2,1)}, bf16[64,4096]{1,0:T(8,128)(2,1)S(1)}, u32[]{:S(2)}, u32[]{:S(2)}) collective-permute-start(bf16[64,4096]{1,0:T(8,128)(2,1)} %bitcast.72), channel_id=1, source_target_pairs={{0,8},{24,16},{1,9},{25,17},{2,10},{26,18},{3,11},{27,19},{4,12},{... | collective-permute-start | bytes 1572872 | tf_op jit(solution)/shard_map/ppermute | solution.py:242
  39.1 25.8 %collective-permute-start.3 = (bf16[64,4096]{1,0:T(8,128)(2,1)}, bf16[64,4096]{1,0:T(8,128)(2,1)}, u32[]{:S(2)}, u32[]{:S(2)}) collective-permute-start(bf16[64,4096]{1,0:T(8,128)(2,1)} %bitcast.71), channel_id=1, source_target_pairs={{0,8},{24,16},{1,9},{25,17},{2,10},{26,18},{3,11},{27,19},{4,12},{... | collective-permute-start | bytes 1572872 | tf_op jit(solution)/shard_map/ppermute | solution.py:242
  52.8 8.1 %copy-start.7 = (bf16[128,1,4096]{2,0,1:T(8,128)(2,1)S(1)}, bf16[128,1,4096]{2,0,1:T(8,128)(2,1)}, u32[]{:S(2)}) copy-start(bf16[128,1,4096]{2,0,1:T(8,128)(2,1)} %param.14) | copy-start | bytes 3145732
  55.5 9.4 %copy-start.2 = (bf16[4,64,4096]{2,1,0:T(8,128)(2,1)S(1)}, bf16[4,64,4096]{2,1,0:T(8,128)(2,1)}, u32[]{:S(2)}) copy-start(bf16[4,64,4096]{2,1,0:T(8,128)(2,1)} %get-tuple-element.17) | copy-start | bytes 6291460
  55.5 15.8 %collective-permute-start.9 = (bf16[64,4096]{1,0:T(8,128)(2,1)}, bf16[64,4096]{1,0:T(8,128)(2,1)}, u32[]{:S(2)}, u32[]{:S(2)}) collective-permute-start(bf16[64,4096]{1,0:T(8,128)(2,1)} %fusion.5), channel_id=1, source_target_pairs={{0,8},{8,16},{1,9},{9,17},{2,10},{10,18},{3,11},{11,19},{4,12},{12... | collective-permute-start | bytes 1572872 | tf_op jit(solution)/shard_map/ppermute | solution.py:245
  56.9 19.2 %collective-permute-start.11 = (bf16[64,4096]{1,0:T(8,128)(2,1)}, bf16[64,4096]{1,0:T(8,128)(2,1)}, u32[]{:S(2)}, u32[]{:S(2)}) collective-permute-start(bf16[64,4096]{1,0:T(8,128)(2,1)} %fusion.5), channel_id=1, source_target_pairs={{24,16},{16,8},{25,17},{17,9},{26,18},{18,10},{27,19},{19,11},{28,... | collective-permute-start | bytes 1572872 | tf_op jit(solution)/shard_map/ppermute | solution.py:246
  61.0 15.1 %copy-start.3 = (bf16[4,64,4096]{2,1,0:T(8,128)(2,1)S(1)}, bf16[4,64,4096]{2,1,0:T(8,128)(2,1)}, u32[]{:S(2)}) copy-start(bf16[4,64,4096]{2,1,0:T(8,128)(2,1)} %get-tuple-element.19) | copy-start | bytes 6291460
  66.0 16.9 %collective-permute-start.4 = (bf16[64,4096]{1,0:T(8,128)(2,1)S(1)}, bf16[64,4096]{1,0:T(8,128)(2,1)S(1)}, u32[]{:S(2)}, u32[]{:S(2)}) collective-permute-start(bf16[64,4096]{1,0:T(8,128)(2,1)S(1)} %fusion.8), channel_id=1, source_target_pairs={{0,8},{8,16},{1,9},{9,17},{2,10},{10,18},{3,11},{11,19},{4,12},{12... | collective-permute-start | bytes 1572872 | tf_op jit(solution)/shard_map/ppermute | solution.py:245
  67.3 19.9 %collective-permute-start.6 = (bf16[64,4096]{1,0:T(8,128)(2,1)S(1)}, bf16[64,4096]{1,0:T(8,128)(2,1)S(1)}, u32[]{:S(2)}, u32[]{:S(2)}) collective-permute-start(bf16[64,4096]{1,0:T(8,128)(2,1)S(1)} %fusion.8), channel_id=1, source_target_pairs={{24,16},{16,8},{25,17},{17,9},{26,18},{18,10},{27,19},{19,11},{28,... | collective-permute-start | bytes 1572872 | tf_op jit(solution)/shard_map/ppermute | solution.py:246
  77.6 20.9 %collective-permute-start.12 = (bf16[64,4096]{1,0:T(8,128)(2,1)S(1)}, bf16[64,4096]{1,0:T(8,128)(2,1)S(1)}, u32[]{:S(2)}, u32[]{:S(2)}) collective-permute-start(bf16[64,4096]{1,0:T(8,128)(2,1)S(1)} %get-tuple-element.24), channel_id=1, source_target_pairs={{24,16},{16,8},{8,0},{25,17},{17,9},{9,1},{26,18},{18,10},{10,2},{... | collective-permute-start | bytes 1572872 | tf_op jit(solution)/shard_map/ppermute | solution.py:246
  79.5 19.0 %collective-permute-start.10 = (bf16[64,4096]{1,0:T(8,128)(2,1)S(1)}, bf16[64,4096]{1,0:T(8,128)(2,1)S(1)}, u32[]{:S(2)}, u32[]{:S(2)}) collective-permute-start(bf16[64,4096]{1,0:T(8,128)(2,1)S(1)} %get-tuple-element.23), channel_id=1, source_target_pairs={{0,8},{8,16},{16,24},{1,9},{9,17},{17,25},{2,10},{10,18},{18,26},{... | collective-permute-start | bytes 1572872 | tf_op jit(solution)/shard_map/ppermute | solution.py:245
  87.5 22.2 %collective-permute-start.7 = (bf16[64,4096]{1,0:T(8,128)(2,1)S(1)}, bf16[64,4096]{1,0:T(8,128)(2,1)S(1)}, u32[]{:S(2)}, u32[]{:S(2)}) collective-permute-start(bf16[64,4096]{1,0:T(8,128)(2,1)S(1)} %get-tuple-element.22), channel_id=1, source_target_pairs={{24,16},{16,8},{8,0},{25,17},{17,9},{9,1},{26,18},{18,10},{10,2},{... | collective-permute-start | bytes 1572872 | tf_op jit(solution)/shard_map/ppermute | solution.py:246
  89.4 20.5 %copy-start.8 = (s32[1,4096]{1,0:T(1,128)S(1)}, s32[1,4096]{1,0:T(1,128)}, u32[]{:S(2)}) copy-start(s32[1,4096]{1,0:T(1,128)} %param.23) | copy-start | bytes 49156
  89.4 20.5 %copy-start.10 = (s32[128]{0:T(128)S(1)}, s32[128]{0:T(128)}, u32[]{:S(2)}) copy-start(s32[128]{0:T(128)} %param.22) | copy-start | bytes 1540
  89.4 20.3 %collective-permute-start.5 = (bf16[64,4096]{1,0:T(8,128)(2,1)S(1)}, bf16[64,4096]{1,0:T(8,128)(2,1)S(1)}, u32[]{:S(2)}, u32[]{:S(2)}) collective-permute-start(bf16[64,4096]{1,0:T(8,128)(2,1)S(1)} %get-tuple-element.21), channel_id=1, source_target_pairs={{0,8},{8,16},{16,24},{1,9},{9,17},{17,25},{2,10},{10,18},{18,26},{... | collective-permute-start | bytes 1572872 | tf_op jit(solution)/shard_map/ppermute | solution.py:245
  (1 other events, 0.8 us)
Sparse Core Ops, SparseCore 0:
  12.4 32.7 all-gather.2

commit v3 on v2

--- a/solution.py
+++ b/solution.py
@@ -15,15 +15,22 @@
 VMEM = 60 * 1024 * 1024
 
 
-def ladder_kernel(sources, targets, live, amps, tiles, out, acc):
+def ladder_kernel(sources, targets, live, place, amps, tiles, out, own, acc):
     step = pl.program_id(0)
     blocks_per_chunk = out.shape[2] // TILE
 
     @pl.when(step == 0)
     def _():
-        @pl.loop(0, acc.shape[0])
+        @pl.loop(0, acc.shape[0], unroll=4)
         def _(b):
             acc[b] = jnp.zeros(acc.shape[1:], jnp.float32)
+
+        start = place[0] * blocks_per_chunk
+
+        @pl.loop(0, blocks_per_chunk, unroll=4)
+        def _(b):
+            columns = pl.ds(pl.multiple_of(b * TILE, TILE), TILE)
+            own[:, columns] = amps[:, pl.ds(pl.multiple_of((start + b) * TILE, TILE), TILE)]
 
     here = jnp.clip(live[0] - step * tiles.shape[0], 0, tiles.shape[0])
 
@@ -51,13 +58,13 @@
     def _():
         for c in range(out.shape[0]):
 
-            @pl.loop(0, blocks_per_chunk)
+            @pl.loop(0, blocks_per_chunk, unroll=4)
             def _(b):
                 columns = pl.ds(pl.multiple_of(b * TILE, TILE), TILE)
                 out[c, :, columns] = acc[c * blocks_per_chunk + b].astype(out.dtype)
 
 
-def ladder_term(amps, tiles, sources, targets, live, chunk_count):
+def ladder_term(amps, tiles, sources, targets, live, place, chunk_count):
     rows, width = amps.shape
     count = tiles.shape[0]
     group = GROUP if count % GROUP == 0 else count
@@ -65,25 +72,31 @@
     return pl.pallas_call(
         ladder_kernel,
         grid_spec=pltpu.PrefetchScalarGridSpec(
-            num_scalar_prefetch=3,
+            num_scalar_prefetch=4,
             grid=(count // group,),
             in_specs=[
-                pl.BlockSpec((rows, width), lambda g, s, t, n: (0, 0)),
+                pl.BlockSpec((rows, width), lambda g, s, t, n, z: (0, 0)),
                 pl.BlockSpec(
                     (group, TILE, TILE),
-                    lambda g, s, t, n: (jnp.minimum(g, jnp.maximum(n[0] - 1, 0) // group), 0, 0),
+                    lambda g, s, t, n, z: (jnp.minimum(g, jnp.maximum(n[0] - 1, 0) // group), 0, 0),
                 ),
             ],
-            out_specs=pl.BlockSpec((chunk_count, rows, chunk), lambda g, s, t, n: (0, 0, 0)),
+            out_specs=[
+                pl.BlockSpec((chunk_count, rows, chunk), lambda g, s, t, n, z: (0, 0, 0)),
+                pl.BlockSpec((rows, chunk), lambda g, s, t, n, z: (0, 0)),
+            ],
             scratch_shapes=[pltpu.VMEM((width // TILE, rows, TILE), jnp.float32)],
         ),
-        out_shape=jax.ShapeDtypeStruct((chunk_count, rows, chunk), jnp.bfloat16),
+        out_shape=[
+            jax.ShapeDtypeStruct((chunk_count, rows, chunk), jnp.bfloat16),
+            jax.ShapeDtypeStruct((rows, chunk), jnp.bfloat16),
+        ],
         compiler_params=pltpu.CompilerParams(vmem_limit_bytes=VMEM),
         cost_estimate=pl.CostEstimate(
             flops=8 * count * rows * TILE * TILE, bytes_accessed=40 * 1024 * 1024, transcendentals=0
         ),
         name="ladder",
-    )(sources, targets, live, amps, tiles)
+    )(sources, targets, live, place, amps, tiles)
 
 
 def cycle_kernel(slots, blocks, targets, chunks, ladder, tiles, *rest):
@@ -91,7 +104,7 @@
     outs = rest[-3 - PIECES : -3]
     pieces = rest[: -3 - PIECES]
     step = pl.program_id(0)
-    blocks_per_chunk = acc.shape[0]
+    blocks_per_chunk = acc.shape[0] - 1
     first = chunks[step] * blocks_per_chunk
     copies = [pltpu.make_async_copy(p, panel.at[j], sems.at[j]) for j, p in enumerate(pieces)]
 
@@ -100,7 +113,7 @@
         for copy in copies:
             copy.start()
 
-    @pl.loop(0, blocks_per_chunk)
+    @pl.loop(0, blocks_per_chunk, unroll=4)
     def _(b):
         columns = pl.ds(pl.multiple_of(b * TILE, TILE), TILE)
         acc[b] = ladder[0, :, columns].astype(jnp.float32)
@@ -110,18 +123,24 @@
         for copy in copies:
             copy.wait()
 
-    @pl.loop(0, tiles.shape[0])
-    def _(t):
+    def product(t):
+        columns = pl.ds(pl.multiple_of(blocks[t] * TILE, TILE), TILE)
+        return jnp.dot(panel[slots[t], :, columns], tiles[t], preferred_element_type=jnp.float32)
+
+    def add(t, value):
         b = targets[t] - first
-
-        @pl.when((b >= 0) & (b < blocks_per_chunk))
-        def _():
-            columns = pl.ds(pl.multiple_of(blocks[t] * TILE, TILE), TILE)
-            acc[b] = acc[b] + jnp.dot(
-                panel[slots[t], :, columns], tiles[t], preferred_element_type=jnp.float32
-            )
-
-    @pl.loop(0, blocks_per_chunk)
+        b = jnp.where((b >= 0) & (b < blocks_per_chunk), b, blocks_per_chunk)
+        acc[b] = acc[b] + value
+
+    unroll = UNROLL if tiles.shape[0] % UNROLL == 0 else 1
+
+    @pl.loop(0, tiles.shape[0] // unroll)
+    def _(g):
+        values = [product(g * unroll + u) for u in range(unroll)]
+        for u in range(unroll):
+            add(g * unroll + u, values[u])
+
+    @pl.loop(0, blocks_per_chunk, unroll=4)
     def _(b):
         columns = pl.ds(pl.multiple_of(b * TILE, TILE), TILE)
         value = acc[b].astype(outs[0].dtype)
@@ -147,7 +166,7 @@
             * PIECES,
             scratch_shapes=[
                 pltpu.VMEM((len(pieces),) + pieces[0].shape, jnp.bfloat16),
-                pltpu.VMEM((chunk // TILE, rows, TILE), jnp.float32),
+                pltpu.VMEM((chunk // TILE + 1, rows, TILE), jnp.float32),
                 pltpu.SemaphoreType.DMA((len(pieces),)),
             ],
         ),
@@ -185,12 +204,16 @@
     me = lax.axis_index("inner")
     amps = amplitudes.reshape(rows, width)
 
-    owned_amps = lax.dynamic_slice(amps, (0, z * owned), (rows, owned))
+    ladder, owned_amps = ladder_term(
+        amps,
+        ladder_tiles,
+        ladder_source[:, 0],
+        ladder_target[:, 0],
+        ladder_live[:, 0],
+        z[None],
+        n,
+    )
     owned_all = lax.all_gather(owned_amps, "row", axis=0, tiled=True)
-
-    ladder = ladder_term(
-        amps, ladder_tiles, ladder_source[:, 0], ladder_target[:, 0], ladder_live[:, 0], n
-    )
 
     held = {0: amps[:, :PANEL]}
     bit = inner_count // 2

time: 119 us -> 117 us (0.983)
  waiting for transfers between devices: 29.4 us -> 32.7 us
  Pallas kernels: 34 us -> 30.9 us
  local copies, waits for them, and re-layouts: 4.75 us -> 2.54 us
    dynamic_slice x1 -> x0, local copies, waits for them, and re-layouts: 2.29 us -> none  [per_device(): owned_amps = lax.dynamic_slice(amps, (0, z * owned), (rows, owned))]
    ppermute x2, waiting for transfers between devices: 2.38 us -> 4.31 us  [per_device(): going[p] = [lax.ppermute(up, 'sec', up_pairs + down_pairs)]]
    pallas_call x1, Pallas kernels: 16 us -> 14.2 us  [ladder_term(): pl.pallas_call(ladder_kernel, grid_spec=pltpu.PrefetchScalarGridSpec(num_...]
    pallas_call x2, Pallas kernels: 18 us -> 16.7 us  [add_cycle(): pl.pallas_call(cycle_kernel, grid_spec=pltpu.PrefetchScalarGridSpec(num_s...]
  transfers between devices with their start and end apart: 14 -> 14, of which waited for: 7 -> 9; matrix products, arithmetic and copies ran while one was open for 9% -> 7% of each run, Pallas kernels for 29% -> 27%
where the time goes in v3:
time: 117 us; the launch traced here: 116 us
  waiting for transfers between devices  32.7 us (28%)
  Pallas kernels  30.9 us (26%)
  starting transfers between devices  25.8 us (22%)
  between operations  14.3 us (12%)
  other arithmetic  7.31 us (6%)
  local copies, waits for them, and re-layouts  2.54 us (2%)
  matrix products  2.19 us (2%)
    ppermute x4, waiting for transfers between devices, per_device(): lax.ppermute(down, 'sec', down_pairs)  25.8 us
    pallas_call x2, Pallas kernels, add_cycle(): pl.pallas_call(cycle_kernel, grid_spec=pltpu.PrefetchScalarGridSpec(num_s...  16.7 us
    pallas_call x1, Pallas kernels, ladder_term(): pl.pallas_call(ladder_kernel, grid_spec=pltpu.PrefetchScalarGridSpec(num_...  14.2 us
    ppermute x4, starting transfers between devices, per_device(): lax.ppermute(down, 'sec', down_pairs)  11.8 us
    ppermute x4, starting transfers between devices, per_device(): lax.ppermute(up, 'sec', up_pairs)  9.48 us
    convert_element_type x4, other arithmetic, plus(): return (a.astype(jnp.float32) + b.astype(jnp.float32)).astype(jnp.bfloat16)  4.86 us
    ppermute x2, waiting for transfers between devices, per_device(): going[p] = [lax.ppermute(up, 'sec', up_pairs + down_pairs)]  4.31 us
    ppermute x2, starting transfers between devices, per_device(): going[p] = [lax.ppermute(up, 'sec', up_pairs + down_pairs)]  2.58 us
  transfers between devices with their start and end apart: 14, of which 9 were waited for; matrix products, arithmetic and copies ran while one was open for 7% of the time, Pallas kernels for 27%

profile of v3, /device:TPU:17, one launch (start us, length us, event | category | flops | bytes accessed | tf_op | source)
XLA Modules:
  0.0 115.8 jit_solution(2261039394942973080)
XLA Ops:
  7.7 1.3 %collective-permute-start = (bf16[128,2048]{1,0:T(8,128)(2,1)S(1)}, bf16[128,2048]{1,0:T(8,128)(2,1)S(1)}, u32[]{:S(2)}, u32[]{:S(2)}) collective-permute-start(bf16[128,2048]{1,0:T(8,128)(2,1)S(1)} %slice.4.rest_0_), channel_id=1, source_target_pairs={{0,2},{1,3},{2,0},{3,1},{4,6},{5,7},{6,4},{7,5},{8,10},{9,11},{10,... | collective-permute-start | bytes 1572872 | tf_op jit(solution)/shard_map/ppermute | solution.py:223
  9.6 14.2 %ladder.1 = (bf16[4,128,4096]{2,1,0:T(8,128)(2,1)}, bf16[128,4096]{1,0:T(8,128)(2,1)}) custom-call(s32[256]{0:T(256)} %bitcast.70, s32[256]{0:T(256)} %bitcast.71, s32[1]{0:T(128)} %bitcast.62.live, s32[1]{0:T(128)} %bitcast.7.place, bf16[128,16384]{1,0:T(8,128)(2,1)} %bitcast.64, bf16[256,128,128]{2,1,0:T(8,128)(2,1)} %tiles.3), custom_call_target="tpu_custom_call" | custom-call | flops 4294967296 | bytes 41943040 | tf_op jit(solution)/shard_map/ladder/pallas_call | solution.py:72
  27.4 6.0 %cycle.2 = (bf16[1,64,4096]{2,1,0:T(8,128)(2,1)}, bf16[1,64,4096]{2,1,0:T(8,128)(2,1)}) custom-call(s32[32]{0:T(128)} %get-tuple-element.30.slots, s32[32]{0:T(128)} %get-tuple-element.29.blocks, s32[32]{0:T(128)} %bitcast.66, s32[1]{0:T(128)} %bitcast.2.chunks, bf16[4,128,4096]{2,1,0:T(8,128)(2,1)} %get-tuple-element.16.ladder, ...), custom_call_target="tpu_custom_call" | custom-call | flops 134217728 | bytes 8388608 | tf_op jit(solution)/shard_map/cycle/pallas_call | solution.py:155
  33.4 1.3 %collective-permute-start.8 = (bf16[64,4096]{1,0:T(8,128)(2,1)}, bf16[64,4096]{1,0:T(8,128)(2,1)S(1)}, u32[]{:S(2)}, u32[]{:S(2)}) collective-permute-start(bf16[64,4096]{1,0:T(8,128)(2,1)} %bitcast.69), channel_id=1, source_target_pairs={{0,8},{24,16},{1,9},{25,17},{2,10},{26,18},{3,11},{27,19},{4,12},{... | collective-permute-start | bytes 1572872 | tf_op jit(solution)/shard_map/ppermute | solution.py:265
  34.7 1.3 %collective-permute-start.3 = (bf16[64,4096]{1,0:T(8,128)(2,1)}, bf16[64,4096]{1,0:T(8,128)(2,1)}, u32[]{:S(2)}, u32[]{:S(2)}) collective-permute-start(bf16[64,4096]{1,0:T(8,128)(2,1)} %bitcast.68), channel_id=1, source_target_pairs={{0,8},{24,16},{1,9},{25,17},{2,10},{26,18},{3,11},{27,19},{4,12},{... | collective-permute-start | bytes 1572872 | tf_op jit(solution)/shard_map/ppermute | solution.py:265
  36.6 10.7 %cycle.3 = (bf16[4,64,4096]{2,1,0:T(8,128)(2,1)}, bf16[4,64,4096]{2,1,0:T(8,128)(2,1)}) custom-call(s32[32]{0:T(128)} %get-tuple-element.30.slots, s32[32]{0:T(128)} %get-tuple-element.29.blocks, s32[32]{0:T(128)} %bitcast.67, s32[4]{0:T(128)} %iota.3.chunks, bf16[4,128,4096]{2,1,0:T(8,128)(2,1)} %get-tuple-element.16.ladder, bf16[32,128,128]{2,1,0:T(8,128)(2,1)} %tiles.5, ...), custom_call_target="tpu_custom_call" | custom-call | flops 134217728 | bytes 8388608 | tf_op jit(solution)/shard_map/cycle/pallas_call | solution.py:155
  47.4 3.8 %collective-permute-done.8 = bf16[64,4096]{1,0:T(8,128)(2,1)S(1)} collective-permute-done((bf16[64,4096]{1,0:T(8,128)(2,1)}, bf16[64,4096]{1,0:T(8,128)(2,1)S(1)}, u32[]{:S(2)}, u32[]{:S(2)}) %collective-permute-start.8) | collective-permute-done | bytes 524320 | tf_op jit(solution)/shard_map/ppermute | solution.py:265
  51.1 2.0 %fusion.4 = bf16[64,4096]{1,0:T(8,128)(2,1)} fusion(bf16[64,4096]{1,0:T(8,128)(2,1)S(1)} %collective-permute-done.8, bf16[4,64,4096]{2,1,0:T(8,128)(2,1)} %get-tuple-element.23, s32[]{:T(128)S(6)} %min.19), kind=kLoop, calls=%fused_computation.8 | loop fusion | flops 1048576 | bytes 1572868 | tf_op jit(solution)/shard_map/convert_element_type | solution.py:246
  53.1 1.4 %collective-permute-start.9 = (bf16[64,4096]{1,0:T(8,128)(2,1)}, bf16[64,4096]{1,0:T(8,128)(2,1)}, u32[]{:S(2)}, u32[]{:S(2)}) collective-permute-start(bf16[64,4096]{1,0:T(8,128)(2,1)} %fusion.4), channel_id=1, source_target_pairs={{0,8},{8,16},{1,9},{9,17},{2,10},{10,18},{3,11},{11,19},{4,12},{12... | collective-permute-start | bytes 1572872 | tf_op jit(solution)/shard_map/ppermute | solution.py:268
  54.5 4.0 %collective-permute-start.11 = (bf16[64,4096]{1,0:T(8,128)(2,1)}, bf16[64,4096]{1,0:T(8,128)(2,1)}, u32[]{:S(2)}, u32[]{:S(2)}) collective-permute-start(bf16[64,4096]{1,0:T(8,128)(2,1)} %fusion.4), channel_id=1, source_target_pairs={{24,16},{16,8},{25,17},{17,9},{26,18},{18,10},{27,19},{19,11},{28,... | collective-permute-start | bytes 1572872 | tf_op jit(solution)/shard_map/ppermute | solution.py:269
  59.6 2.2 %fusion = f32[128,4096]{1,0:T(8,128)S(1)} fusion(bf16[128,256]{1,0:T(8,128)(2,1)S(1)} %copy-done, bf16[256,4096]{1,0:T(8,128)(2,1)} %all-gather.2.cloned.1.call-done, bf16[128,1,4096]{2,0,1:T(8,128)(2,1)S(1)} %copy-done.7), kind=kOutput, calls=%fused_computation.1 | convolution fusion | flops 269484032 | bytes 5308416 | tf_op jit(solution)/shard_map/dot_general | solution.py:239
  62.4 1.2 %fusion.7 = bf16[64,4096]{1,0:T(8,128)(2,1)S(1)} fusion(bf16[64,4096]{1,0:T(8,128)(2,1)} %collective-permute-done.3, bf16[4,64,4096]{2,1,0:T(8,128)(2,1)S(1)} %copy-done.2, s32[]{:T(128)S(6)} %min.19), kind=kLoop, calls=%fused_computation.15 | loop fusion | flops 1048576 | bytes 1572868 | tf_op jit(solution)/shard_map/convert_element_type | solution.py:246
  63.5 1.3 %collective-permute-start.4 = (bf16[64,4096]{1,0:T(8,128)(2,1)S(1)}, bf16[64,4096]{1,0:T(8,128)(2,1)S(1)}, u32[]{:S(2)}, u32[]{:S(2)}) collective-permute-start(bf16[64,4096]{1,0:T(8,128)(2,1)S(1)} %fusion.7), channel_id=1, source_target_pairs={{0,8},{8,16},{1,9},{9,17},{2,10},{10,18},{3,11},{11,19},{4,12},{12... | collective-permute-start | bytes 1572872 | tf_op jit(solution)/shard_map/ppermute | solution.py:268
  64.8 4.0 %collective-permute-start.6 = (bf16[64,4096]{1,0:T(8,128)(2,1)S(1)}, bf16[64,4096]{1,0:T(8,128)(2,1)S(1)}, u32[]{:S(2)}, u32[]{:S(2)}) collective-permute-start(bf16[64,4096]{1,0:T(8,128)(2,1)S(1)} %fusion.7), channel_id=1, source_target_pairs={{24,16},{16,8},{25,17},{17,9},{26,18},{18,10},{27,19},{19,11},{28,... | collective-permute-start | bytes 1572872 | tf_op jit(solution)/shard_map/ppermute | solution.py:269
  68.9 4.8 %collective-permute-done.11 = bf16[64,4096]{1,0:T(8,128)(2,1)} collective-permute-done((bf16[64,4096]{1,0:T(8,128)(2,1)}, bf16[64,4096]{1,0:T(8,128)(2,1)}, u32[]{:S(2)}, u32[]{:S(2)}) %collective-permute-start.11) | collective-permute-done | bytes 524320 | tf_op jit(solution)/shard_map/ppermute | solution.py:269
  73.6 1.5 %fusion.5 = (bf16[64,4096]{1,0:T(8,128)(2,1)S(1)}, bf16[64,4096]{1,0:T(8,128)(2,1)S(1)}) fusion(bf16[64,4096]{1,0:T(8,128)(2,1)} %collective-permute-done.9, bf16[4,64,4096]{2,1,0:T(8,128)(2,1)S(1)} %copy-done.3, s32[]{:T(128)S(6)} %min.18, bf16[64,4096]{1,0:T(8,128)(2,1)} %collective-permute-done.11, s32[]{:T(128)S(6)} %min.20), kind=kLoop, calls=%fused_computation.10 | loop fusion | flops 2097152 | bytes 3145736 | tf_op jit(solution)/shard_map/convert_element_type | solution.py:246
  75.1 1.9 %collective-permute-start.12 = (bf16[64,4096]{1,0:T(8,128)(2,1)S(1)}, bf16[64,4096]{1,0:T(8,128)(2,1)S(1)}, u32[]{:S(2)}, u32[]{:S(2)}) collective-permute-start(bf16[64,4096]{1,0:T(8,128)(2,1)S(1)} %get-tuple-element.28), channel_id=1, source_target_pairs={{24,16},{16,8},{8,0},{25,17},{17,9},{9,1},{26,18},{18,10},{10,2},{... | collective-permute-start | bytes 1572872 | tf_op jit(solution)/shard_map/ppermute | solution.py:269
  77.0 3.4 %collective-permute-start.10 = (bf16[64,4096]{1,0:T(8,128)(2,1)S(1)}, bf16[64,4096]{1,0:T(8,128)(2,1)S(1)}, u32[]{:S(2)}, u32[]{:S(2)}) collective-permute-start(bf16[64,4096]{1,0:T(8,128)(2,1)S(1)} %get-tuple-element.27), channel_id=1, source_target_pairs={{0,8},{8,16},{16,24},{1,9},{9,17},{17,25},{2,10},{10,18},{18,26},{... | collective-permute-start | bytes 1572872 | tf_op jit(solution)/shard_map/ppermute | solution.py:268
  80.4 4.3 %collective-permute-done.6 = bf16[64,4096]{1,0:T(8,128)(2,1)S(1)} collective-permute-done((bf16[64,4096]{1,0:T(8,128)(2,1)S(1)}, bf16[64,4096]{1,0:T(8,128)(2,1)S(1)}, u32[]{:S(2)}, u32[]{:S(2)}) %collective-permute-start.6) | collective-permute-done | bytes 524320 | tf_op jit(solution)/shard_map/ppermute | solution.py:269
  85.0 1.9 %collective-permute-start.7 = (bf16[64,4096]{1,0:T(8,128)(2,1)S(1)}, bf16[64,4096]{1,0:T(8,128)(2,1)S(1)}, u32[]{:S(2)}, u32[]{:S(2)}) collective-permute-start(bf16[64,4096]{1,0:T(8,128)(2,1)S(1)} %get-tuple-element.26), channel_id=1, source_target_pairs={{24,16},{16,8},{8,0},{25,17},{17,9},{9,1},{26,18},{18,10},{10,2},{... | collective-permute-start | bytes 1572872 | tf_op jit(solution)/shard_map/ppermute | solution.py:269
  87.0 3.4 %collective-permute-start.5 = (bf16[64,4096]{1,0:T(8,128)(2,1)S(1)}, bf16[64,4096]{1,0:T(8,128)(2,1)S(1)}, u32[]{:S(2)}, u32[]{:S(2)}) collective-permute-start(bf16[64,4096]{1,0:T(8,128)(2,1)S(1)} %get-tuple-element.25), channel_id=1, source_target_pairs={{0,8},{8,16},{16,24},{1,9},{9,17},{17,25},{2,10},{10,18},{18,26},{... | collective-permute-start | bytes 1572872 | tf_op jit(solution)/shard_map/ppermute | solution.py:268
  90.4 5.6 %collective-permute-done.12 = bf16[64,4096]{1,0:T(8,128)(2,1)S(1)} collective-permute-done((bf16[64,4096]{1,0:T(8,128)(2,1)S(1)}, bf16[64,4096]{1,0:T(8,128)(2,1)S(1)}, u32[]{:S(2)}, u32[]{:S(2)}) %collective-permute-start.12) | collective-permute-done | bytes 524320 | tf_op jit(solution)/shard_map/ppermute | solution.py:269
  96.2 11.1 %collective-permute-done.7 = bf16[64,4096]{1,0:T(8,128)(2,1)S(1)} collective-permute-done((bf16[64,4096]{1,0:T(8,128)(2,1)S(1)}, bf16[64,4096]{1,0:T(8,128)(2,1)S(1)}, u32[]{:S(2)}, u32[]{:S(2)}) %collective-permute-start.7) | collective-permute-done | bytes 524320 | tf_op jit(solution)/shard_map/ppermute | solution.py:269
  107.4 1.5 %fusion.9 = bf16[128,1,4096]{2,0,1:T(8,128)(2,1)} fusion(s32[4096]{0:T(1024)S(1)} %bitcast.65, s32[128]{0:T(128)S(1)} %copy-done.10, f32[128,4096]{1,0:T(8,128)S(1)} %fusion, f32[64,4096]{1,0:T(8,128)S(1)} %convert_add_fusion.3, f32[64,4096]{1,0:T(8,128)S(1)} %convert_add_fusion.7), kind=kLoop, calls=%fused_computation.19 | loop fusion | flops 3670016 | bytes 5259776 | tf_op jit(solution)/shard_map/reshape | solution.py:281
  (41 shorter events, 7.5 us)
Async XLA Ops:
  6.5 53.1 %copy-start = (bf16[128,256]{1,0:T(8,128)(2,1)S(1)}, bf16[128,256]{1,0:T(8,128)(2,1)}, u32[]{:S(2)}) copy-start(bf16[128,256]{1,0:T(8,128)(2,1)} %param.13) | copy-start | bytes 196612
  6.5 53.1 %all-gather.2.cloned.1.call-start = ((), (), s32[]{:S(2)}) async-start(), calls=%async_computation | async-start | bytes 3145728 | tf_op jit(solution)/shard_map/all_gather | solution.py:216
  7.7 16.2 %copy-start.1 = (bf16[128,2048]{1,0:T(8,128)(2,1)}, bf16[128,2048]{1,0:T(8,128)(2,1)S(1)}, u32[]{:S(2)}) copy-start(bf16[128,2048]{1,0:T(8,128)(2,1)S(1)} %slice.4.rest_0_) | copy-start | bytes 1572868
  7.7 16.3 %collective-permute-start = (bf16[128,2048]{1,0:T(8,128)(2,1)S(1)}, bf16[128,2048]{1,0:T(8,128)(2,1)S(1)}, u32[]{:S(2)}, u32[]{:S(2)}) collective-permute-start(bf16[128,2048]{1,0:T(8,128)(2,1)S(1)} %slice.4.rest_0_), channel_id=1, source_target_pairs={{0,2},{1,3},{2,0},{3,1},{4,6},{5,7},{6,4},{7,5},{8,10},{9,11},{10,... | collective-permute-start | bytes 1572872 | tf_op jit(solution)/shard_map/ppermute | solution.py:223
  9.6 14.9 %copy-start.9 = (s32[32,1]{0,1:T(1,128)S(1)}, s32[32,1]{0,1:T(1,128)}, u32[]{:S(2)}) copy-start(s32[32,1]{0,1:T(1,128)} %param.20) | copy-start | bytes 388
  23.9 2.0 %collective-permute-start.1 = (bf16[128,2048]{1,0:T(8,128)(2,1)S(1)}, bf16[128,2048]{1,0:T(8,128)(2,1)S(1)}, u32[]{:S(2)}, u32[]{:S(2)}) collective-permute-start(bf16[128,2048]{1,0:T(8,128)(2,1)S(1)} %slice.4.rest_0_), channel_id=1, source_target_pairs={{0,1},{1,0},{2,3},{3,2},{4,5},{5,4},{6,7},{7,6},{8,9},{9,8},{10,11... | collective-permute-start | bytes 1572872 | tf_op jit(solution)/shard_map/ppermute | solution.py:223
  24.0 2.6 %copy-start.4 = (bf16[128,2048]{1,0:T(8,128)(2,1)}, bf16[128,2048]{1,0:T(8,128)(2,1)S(1)}, u32[]{:S(2)}) copy-start(bf16[128,2048]{1,0:T(8,128)(2,1)S(1)} %collective-permute-done.rest_2_) | copy-start | bytes 1572868
  24.0 2.6 %collective-permute-start.2 = (bf16[128,2048]{1,0:T(8,128)(2,1)S(1)}, bf16[128,2048]{1,0:T(8,128)(2,1)S(1)}, u32[]{:S(2)}, u32[]{:S(2)}) collective-permute-start(bf16[128,2048]{1,0:T(8,128)(2,1)S(1)} %collective-permute-done.rest_2_), channel_id=1, source_target_pairs={{0,1},{1,0},{2,3},{3,2},{4,5},{5,4},{6,7},{7,6},{8,9},{9,8},{10,11... | collective-permute-start | bytes 1572872 | tf_op jit(solution)/shard_map/ppermute | solution.py:223
  26.6 0.8 copy-start.6
  33.4 17.7 %collective-permute-start.8 = (bf16[64,4096]{1,0:T(8,128)(2,1)}, bf16[64,4096]{1,0:T(8,128)(2,1)S(1)}, u32[]{:S(2)}, u32[]{:S(2)}) collective-permute-start(bf16[64,4096]{1,0:T(8,128)(2,1)} %bitcast.69), channel_id=1, source_target_pairs={{0,8},{24,16},{1,9},{25,17},{2,10},{26,18},{3,11},{27,19},{4,12},{... | collective-permute-start | bytes 1572872 | tf_op jit(solution)/shard_map/ppermute | solution.py:265
  34.7 27.6 %collective-permute-start.3 = (bf16[64,4096]{1,0:T(8,128)(2,1)}, bf16[64,4096]{1,0:T(8,128)(2,1)}, u32[]{:S(2)}, u32[]{:S(2)}) collective-permute-start(bf16[64,4096]{1,0:T(8,128)(2,1)} %bitcast.68), channel_id=1, source_target_pairs={{0,8},{24,16},{1,9},{25,17},{2,10},{26,18},{3,11},{27,19},{4,12},{... | collective-permute-start | bytes 1572872 | tf_op jit(solution)/shard_map/ppermute | solution.py:265
  47.4 12.3 %copy-start.7 = (bf16[128,1,4096]{2,0,1:T(8,128)(2,1)S(1)}, bf16[128,1,4096]{2,0,1:T(8,128)(2,1)}, u32[]{:S(2)}) copy-start(bf16[128,1,4096]{2,0,1:T(8,128)(2,1)} %param.14) | copy-start | bytes 3145732
  53.1 9.3 %copy-start.2 = (bf16[4,64,4096]{2,1,0:T(8,128)(2,1)S(1)}, bf16[4,64,4096]{2,1,0:T(8,128)(2,1)}, u32[]{:S(2)}) copy-start(bf16[4,64,4096]{2,1,0:T(8,128)(2,1)} %get-tuple-element.21) | copy-start | bytes 6291460
  53.1 15.7 %collective-permute-start.9 = (bf16[64,4096]{1,0:T(8,128)(2,1)}, bf16[64,4096]{1,0:T(8,128)(2,1)}, u32[]{:S(2)}, u32[]{:S(2)}) collective-permute-start(bf16[64,4096]{1,0:T(8,128)(2,1)} %fusion.4), channel_id=1, source_target_pairs={{0,8},{8,16},{1,9},{9,17},{2,10},{10,18},{3,11},{11,19},{4,12},{12... | collective-permute-start | bytes 1572872 | tf_op jit(solution)/shard_map/ppermute | solution.py:268
  54.5 19.1 %collective-permute-start.11 = (bf16[64,4096]{1,0:T(8,128)(2,1)}, bf16[64,4096]{1,0:T(8,128)(2,1)}, u32[]{:S(2)}, u32[]{:S(2)}) collective-permute-start(bf16[64,4096]{1,0:T(8,128)(2,1)} %fusion.4), channel_id=1, source_target_pairs={{24,16},{16,8},{25,17},{17,9},{26,18},{18,10},{27,19},{19,11},{28,... | collective-permute-start | bytes 1572872 | tf_op jit(solution)/shard_map/ppermute | solution.py:269
  59.6 14.0 %copy-start.3 = (bf16[4,64,4096]{2,1,0:T(8,128)(2,1)S(1)}, bf16[4,64,4096]{2,1,0:T(8,128)(2,1)}, u32[]{:S(2)}) copy-start(bf16[4,64,4096]{2,1,0:T(8,128)(2,1)} %get-tuple-element.23) | copy-start | bytes 6291460
  63.5 16.9 %collective-permute-start.4 = (bf16[64,4096]{1,0:T(8,128)(2,1)S(1)}, bf16[64,4096]{1,0:T(8,128)(2,1)S(1)}, u32[]{:S(2)}, u32[]{:S(2)}) collective-permute-start(bf16[64,4096]{1,0:T(8,128)(2,1)S(1)} %fusion.7), channel_id=1, source_target_pairs={{0,8},{8,16},{1,9},{9,17},{2,10},{10,18},{3,11},{11,19},{4,12},{12... | collective-permute-start | bytes 1572872 | tf_op jit(solution)/shard_map/ppermute | solution.py:268
  64.8 19.9 %collective-permute-start.6 = (bf16[64,4096]{1,0:T(8,128)(2,1)S(1)}, bf16[64,4096]{1,0:T(8,128)(2,1)S(1)}, u32[]{:S(2)}, u32[]{:S(2)}) collective-permute-start(bf16[64,4096]{1,0:T(8,128)(2,1)S(1)} %fusion.7), channel_id=1, source_target_pairs={{24,16},{16,8},{25,17},{17,9},{26,18},{18,10},{27,19},{19,11},{28,... | collective-permute-start | bytes 1572872 | tf_op jit(solution)/shard_map/ppermute | solution.py:269
  75.1 20.9 %collective-permute-start.12 = (bf16[64,4096]{1,0:T(8,128)(2,1)S(1)}, bf16[64,4096]{1,0:T(8,128)(2,1)S(1)}, u32[]{:S(2)}, u32[]{:S(2)}) collective-permute-start(bf16[64,4096]{1,0:T(8,128)(2,1)S(1)} %get-tuple-element.28), channel_id=1, source_target_pairs={{24,16},{16,8},{8,0},{25,17},{17,9},{9,1},{26,18},{18,10},{10,2},{... | collective-permute-start | bytes 1572872 | tf_op jit(solution)/shard_map/ppermute | solution.py:269
  77.0 19.0 %collective-permute-start.10 = (bf16[64,4096]{1,0:T(8,128)(2,1)S(1)}, bf16[64,4096]{1,0:T(8,128)(2,1)S(1)}, u32[]{:S(2)}, u32[]{:S(2)}) collective-permute-start(bf16[64,4096]{1,0:T(8,128)(2,1)S(1)} %get-tuple-element.27), channel_id=1, source_target_pairs={{0,8},{8,16},{16,24},{1,9},{9,17},{17,25},{2,10},{10,18},{18,26},{... | collective-permute-start | bytes 1572872 | tf_op jit(solution)/shard_map/ppermute | solution.py:268
  85.0 22.2 %collective-permute-start.7 = (bf16[64,4096]{1,0:T(8,128)(2,1)S(1)}, bf16[64,4096]{1,0:T(8,128)(2,1)S(1)}, u32[]{:S(2)}, u32[]{:S(2)}) collective-permute-start(bf16[64,4096]{1,0:T(8,128)(2,1)S(1)} %get-tuple-element.26), channel_id=1, source_target_pairs={{24,16},{16,8},{8,0},{25,17},{17,9},{9,1},{26,18},{18,10},{10,2},{... | collective-permute-start | bytes 1572872 | tf_op jit(solution)/shard_map/ppermute | solution.py:269
  86.9 20.5 %copy-start.8 = (s32[1,4096]{1,0:T(1,128)S(1)}, s32[1,4096]{1,0:T(1,128)}, u32[]{:S(2)}) copy-start(s32[1,4096]{1,0:T(1,128)} %param.23) | copy-start | bytes 49156
  86.9 20.5 %copy-start.10 = (s32[128]{0:T(128)S(1)}, s32[128]{0:T(128)}, u32[]{:S(2)}) copy-start(s32[128]{0:T(128)} %param.22) | copy-start | bytes 1540
  87.0 20.3 %collective-permute-start.5 = (bf16[64,4096]{1,0:T(8,128)(2,1)S(1)}, bf16[64,4096]{1,0:T(8,128)(2,1)S(1)}, u32[]{:S(2)}, u32[]{:S(2)}) collective-permute-start(bf16[64,4096]{1,0:T(8,128)(2,1)S(1)} %get-tuple-element.25), channel_id=1, source_target_pairs={{0,8},{8,16},{16,24},{1,9},{9,17},{17,25},{2,10},{10,18},{18,26},{... | collective-permute-start | bytes 1572872 | tf_op jit(solution)/shard_map/ppermute | solution.py:268
  (1 other events, 0.8 us)
Sparse Core Ops, SparseCore 0:
  24.0 35.5 all-gather.1

commit v4 on v3

--- a/solution.py
+++ b/solution.py
@@ -15,16 +15,22 @@
 VMEM = 60 * 1024 * 1024
 
 
-def ladder_kernel(sources, targets, live, place, amps, tiles, out, own, acc):
+def ladder_kernel(
+    sources, targets, live, place, amps_in, tiles, out_all, own, amps, out, acc, in_sem, out_sems
+):
     step = pl.program_id(0)
+    fetch = pltpu.make_async_copy(amps_in, amps, in_sem)
     blocks_per_chunk = out.shape[2] // TILE
 
     @pl.when(step == 0)
     def _():
+        fetch.start()
+
         @pl.loop(0, acc.shape[0], unroll=4)
         def _(b):
             acc[b] = jnp.zeros(acc.shape[1:], jnp.float32)
 
+        fetch.wait()
         start = place[0] * blocks_per_chunk
 
         @pl.loop(0, blocks_per_chunk, unroll=4)
@@ -56,12 +62,18 @@
 
     @pl.when(step == pl.num_programs(0) - 1)
     def _():
+        writes = []
         for c in range(out.shape[0]):
 
             @pl.loop(0, blocks_per_chunk, unroll=4)
             def _(b):
                 columns = pl.ds(pl.multiple_of(b * TILE, TILE), TILE)
                 out[c, :, columns] = acc[c * blocks_per_chunk + b].astype(out.dtype)
+
+            writes.append(pltpu.make_async_copy(out.at[c], out_all.at[c], out_sems.at[c]))
+            writes[c].start()
+        for write in writes:
+            write.wait()
 
 
 def ladder_term(amps, tiles, sources, targets, live, place, chunk_count):
@@ -75,17 +87,23 @@
             num_scalar_prefetch=4,
             grid=(count // group,),
             in_specs=[
-                pl.BlockSpec((rows, width), lambda g, s, t, n, z: (0, 0)),
+                pl.BlockSpec(memory_space=pl.ANY),
                 pl.BlockSpec(
                     (group, TILE, TILE),
                     lambda g, s, t, n, z: (jnp.minimum(g, jnp.maximum(n[0] - 1, 0) // group), 0, 0),
                 ),
             ],
             out_specs=[
-                pl.BlockSpec((chunk_count, rows, chunk), lambda g, s, t, n, z: (0, 0, 0)),
+                pl.BlockSpec(memory_space=pl.ANY),
                 pl.BlockSpec((rows, chunk), lambda g, s, t, n, z: (0, 0)),
             ],
-            scratch_shapes=[pltpu.VMEM((width // TILE, rows, TILE), jnp.float32)],
+            scratch_shapes=[
+                pltpu.VMEM((rows, width), jnp.bfloat16),
+                pltpu.VMEM((chunk_count, rows, chunk), jnp.bfloat16),
+                pltpu.VMEM((width // TILE, rows, TILE), jnp.float32),
+                pltpu.SemaphoreType.DMA,
+                pltpu.SemaphoreType.DMA((chunk_count,)),
+            ],
         ),
         out_shape=[
             jax.ShapeDtypeStruct((chunk_count, rows, chunk), jnp.bfloat16),
@@ -99,14 +117,18 @@
     )(sources, targets, live, place, amps, tiles)
 
 
-def cycle_kernel(slots, blocks, targets, chunks, ladder, tiles, *rest):
-    panel, acc, sems = rest[-3:]
-    outs = rest[-3 - PIECES : -3]
-    pieces = rest[: -3 - PIECES]
+def cycle_kernel(part, outputs, slots, blocks, targets, chunks, ladder, tiles_in, *rest):
+    panel, tiles, acc, tile_sem, sems = rest[-5:]
+    outs = rest[-5 - outputs : -5]
+    pieces = rest[: -5 - outputs]
     step = pl.program_id(0)
     blocks_per_chunk = acc.shape[0] - 1
     first = chunks[step] * blocks_per_chunk
-    copies = [pltpu.make_async_copy(p, panel.at[j], sems.at[j]) for j, p in enumerate(pieces)]
+    rows = panel.shape[1]
+    copies = [pltpu.make_async_copy(tiles_in, tiles, tile_sem)] + [
+        pltpu.make_async_copy(p.at[pl.ds(part * rows, rows)], panel.at[j], sems.at[j])
+        for j, p in enumerate(pieces)
+    ]
 
     @pl.when(step == 0)
     def _():
@@ -145,32 +167,36 @@
         columns = pl.ds(pl.multiple_of(b * TILE, TILE), TILE)
         value = acc[b].astype(outs[0].dtype)
         cut = outs[0].shape[1]
-        for p in range(PIECES):
+        for p in range(outputs):
             outs[p][0, :, columns] = value[p * cut : (p + 1) * cut]
 
 
-def add_cycle(ladder, tiles, pieces, slots, blocks, targets, chunks):
+def add_cycle(ladder, tiles, pieces, slots, blocks, targets, chunks, part=None):
     _, rows, chunk = ladder.shape
     count = chunks.shape[0]
+    cut = rows // PIECES
+    outputs = PIECES if part is None else 1
+    if part is None:
+        part = 0
+    else:
+        rows = cut
     return pl.pallas_call(
-        cycle_kernel,
+        functools.partial(cycle_kernel, part, outputs),
         grid_spec=pltpu.PrefetchScalarGridSpec(
             num_scalar_prefetch=4,
             grid=(count,),
-            in_specs=[
-                pl.BlockSpec((1, rows, chunk), lambda i, s, b, t, c: (c[i], 0, 0)),
-                pl.BlockSpec(tiles.shape, lambda i, s, b, t, c: (0, 0, 0)),
-            ]
-            + [pl.BlockSpec(memory_space=pl.ANY)] * len(pieces),
-            out_specs=[pl.BlockSpec((1, rows // PIECES, chunk), lambda i, s, b, t, c: (i, 0, 0))]
-            * PIECES,
+            in_specs=[pl.BlockSpec((1, rows, chunk), lambda i, s, b, t, c: (c[i], part, 0))]
+            + [pl.BlockSpec(memory_space=pl.ANY)] * (1 + len(pieces)),
+            out_specs=[pl.BlockSpec((1, cut, chunk), lambda i, s, b, t, c: (i, 0, 0))] * outputs,
             scratch_shapes=[
-                pltpu.VMEM((len(pieces),) + pieces[0].shape, jnp.bfloat16),
+                pltpu.VMEM((len(pieces), rows, pieces[0].shape[1]), jnp.bfloat16),
+                pltpu.VMEM(tiles.shape, jnp.bfloat16),
                 pltpu.VMEM((chunk // TILE + 1, rows, TILE), jnp.float32),
+                pltpu.SemaphoreType.DMA,
                 pltpu.SemaphoreType.DMA((len(pieces),)),
             ],
         ),
-        out_shape=[jax.ShapeDtypeStruct((count, rows // PIECES, chunk), jnp.bfloat16)] * PIECES,
+        out_shape=[jax.ShapeDtypeStruct((count, cut, chunk), jnp.bfloat16)] * outputs,
         compiler_params=pltpu.CompilerParams(vmem_limit_bytes=VMEM),
         cost_estimate=pl.CostEstimate(
             flops=2 * tiles.shape[0] * rows * TILE * TILE,
@@ -233,7 +259,7 @@
 
     finish = functools.partial(add_cycle, ladder, cycle_tiles, pieces, slots, blocks, targets)
     edge = jnp.where(z == 0, n - 1, 0).astype(jnp.int32)
-    first_shares = finish(edge[None])
+    first_shares = [finish(edge[None], part=p)[0] for p in range(PIECES)]
     shares = finish(jnp.arange(n, dtype=jnp.int32))
 
     hole = jnp.dot(hole_ladder, owned_all, preferred_element_type=jnp.float32)

time: 117 us -> 118 us (level)
  waiting for transfers between devices: 32.7 us -> 26.2 us
  Pallas kernels: 30.9 us -> 36.6 us
    ppermute x4, waiting for transfers between devices: 25.8 us -> 21.3 us  [per_device(): lax.ppermute(down, 'sec', down_pairs)]
    pallas_call x2 -> x3, Pallas kernels: 16.7 us -> 21 us  [add_cycle(): pl.pallas_call(functools.partial(cycle_kernel, part, outputs), grid_spec=...]
    ppermute x2, waiting for transfers between devices: 4.31 us -> 0.01 us  [per_device(): going[p] = [lax.ppermute(up, 'sec', up_pairs + down_pairs)]]
    ppermute x4, waiting for transfers between devices: 0.01 us -> 3.29 us  [per_device(): lax.ppermute(up, 'sec', up_pairs)]
    ppermute x4, starting transfers between devices: 11.8 us -> 13.3 us  [per_device(): lax.ppermute(down, 'sec', down_pairs)]
    ppermute x4, starting transfers between devices: 9.48 us -> 8.03 us  [per_device(): lax.ppermute(up, 'sec', up_pairs)]
    pallas_call x1, Pallas kernels: 14.2 us -> 15.6 us  [ladder_term(): pl.pallas_call(ladder_kernel, grid_spec=pltpu.PrefetchScalarGridSpec(num_...]
  transfers between devices with their start and end apart: 14 -> 14, of which waited for: 9 -> 8; matrix products, arithmetic and copies ran while one was open for 7% -> 7% of each run, Pallas kernels for 27% -> 32%
where the time goes in v4:
time: 118 us; the launch traced here: 116 us
  Pallas kernels  36.6 us (31%)
  starting transfers between devices  26.8 us (23%)
  waiting for transfers between devices  26.2 us (22%)
  between operations  14.3 us (12%)
  other arithmetic  7.48 us (6%)
  local copies, waits for them, and re-layouts  2.47 us (2%)
  matrix products  2.19 us (2%)
    ppermute x4, waiting for transfers between devices, per_device(): lax.ppermute(down, 'sec', down_pairs)  21.3 us
    pallas_call x3, Pallas kernels, add_cycle(): pl.pallas_call(functools.partial(cycle_kernel, part, outputs), grid_spec=...  21 us
    pallas_call x1, Pallas kernels, ladder_term(): pl.pallas_call(ladder_kernel, grid_spec=pltpu.PrefetchScalarGridSpec(num_...  15.6 us
    ppermute x4, starting transfers between devices, per_device(): lax.ppermute(down, 'sec', down_pairs)  13.3 us
    ppermute x4, starting transfers between devices, per_device(): lax.ppermute(up, 'sec', up_pairs)  8.03 us
    convert_element_type x4, other arithmetic, plus(): return (a.astype(jnp.float32) + b.astype(jnp.float32)).astype(jnp.bfloat16)  4.96 us
    ppermute x4, waiting for transfers between devices, per_device(): lax.ppermute(up, 'sec', up_pairs)  3.29 us
    ppermute x3, starting transfers between devices, per_device(): held[j ^ bit] = lax.ppermute(held[j], 'inner', pairs)  2.88 us
  transfers between devices with their start and end apart: 14, of which 8 were waited for; matrix products, arithmetic and copies ran while one was open for 7% of the time, Pallas kernels for 32%

profile of v4, /device:TPU:17, one launch (start us, length us, event | category | flops | bytes accessed | tf_op | source)
XLA Modules:
  0.0 116.0 jit_solution(17646017195807462253)
XLA Ops:
  7.7 1.3 %collective-permute-start = (bf16[128,2048]{1,0:T(8,128)(2,1)S(1)}, bf16[128,2048]{1,0:T(8,128)(2,1)S(1)}, u32[]{:S(2)}, u32[]{:S(2)}) collective-permute-start(bf16[128,2048]{1,0:T(8,128)(2,1)S(1)} %slice.4.rest_0_), channel_id=1, source_target_pairs={{0,2},{1,3},{2,0},{3,1},{4,6},{5,7},{6,4},{7,5},{8,10},{9,11},{10,... | collective-permute-start | bytes 1572872 | tf_op jit(solution)/shard_map/ppermute | solution.py:249
  9.6 15.6 %ladder.1 = (bf16[4,128,4096]{2,1,0:T(8,128)(2,1)}, bf16[128,4096]{1,0:T(8,128)(2,1)}) custom-call(s32[256]{0:T(256)} %bitcast.71, s32[256]{0:T(256)} %bitcast.72, s32[1]{0:T(128)} %bitcast.62.live, s32[1]{0:T(128)} %bitcast.7.place, bf16[128,16384]{1,0:T(8,128)(2,1)} %bitcast.66, bf16[256,128,128]{2,1,0:T(8,128)(2,1)} %tiles.1), custom_call_target="tpu_custom_call" | custom-call | flops 4294967296 | bytes 41943040 | tf_op jit(solution)/shard_map/ladder/pallas_call | solution.py:84
  25.2 1.5 %collective-permute-start.1 = (bf16[128,2048]{1,0:T(8,128)(2,1)S(1)}, bf16[128,2048]{1,0:T(8,128)(2,1)S(1)}, u32[]{:S(2)}, u32[]{:S(2)}) collective-permute-start(bf16[128,2048]{1,0:T(8,128)(2,1)S(1)} %slice.4.rest_0_), channel_id=1, source_target_pairs={{0,1},{1,0},{2,3},{3,2},{4,5},{5,4},{6,7},{7,6},{8,9},{9,8},{10,11... | collective-permute-start | bytes 1572872 | tf_op jit(solution)/shard_map/ppermute | solution.py:249
  29.8 5.3 %cycle.5 = bf16[1,64,4096]{2,1,0:T(8,128)(2,1)} custom-call(s32[32]{0:T(128)} %get-tuple-element.26.slots, s32[32]{0:T(128)} %get-tuple-element.25.blocks, s32[32]{0:T(128)} %bitcast.68, s32[1]{0:T(128)} %bitcast.2.chunks, bf16[4,128,4096]{2,1,0:T(8,128)(2,1)} %get-tuple-element.14.ladder, bf16[32,128,128]{2,1,0:T(8,128)(2,1)} %tiles_in.5, ...), custom_call_target="tpu_custom_call" | custom-call | flops 67108864 | bytes 8388608 | tf_op jit(solution)/shard_map/cycle/pallas_call | solution.py:183
  35.1 1.3 %collective-permute-start.8 = (bf16[64,4096]{1,0:T(8,128)(2,1)}, bf16[64,4096]{1,0:T(8,128)(2,1)S(1)}, u32[]{:S(2)}, u32[]{:S(2)}) collective-permute-start(bf16[64,4096]{1,0:T(8,128)(2,1)} %bitcast.63), channel_id=1, source_target_pairs={{0,8},{24,16},{1,9},{25,17},{2,10},{26,18},{3,11},{27,19},{4,12},{... | collective-permute-start | bytes 1572872 | tf_op jit(solution)/shard_map/ppermute | solution.py:291
  36.4 5.0 %cycle.3 = bf16[1,64,4096]{2,1,0:T(8,128)(2,1)} custom-call(s32[32]{0:T(128)} %get-tuple-element.26.slots, s32[32]{0:T(128)} %get-tuple-element.25.blocks, s32[32]{0:T(128)} %bitcast.69, s32[1]{0:T(128)} %bitcast.2.chunks, bf16[4,128,4096]{2,1,0:T(8,128)(2,1)} %get-tuple-element.14.ladder, bf16[32,128,128]{2,1,0:T(8,128)(2,1)} %tiles_in.5, ...), custom_call_target="tpu_custom_call" | custom-call | flops 67108864 | bytes 8388608 | tf_op jit(solution)/shard_map/cycle/pallas_call | solution.py:183
  41.4 1.3 %collective-permute-start.3 = (bf16[64,4096]{1,0:T(8,128)(2,1)}, bf16[64,4096]{1,0:T(8,128)(2,1)}, u32[]{:S(2)}, u32[]{:S(2)}) collective-permute-start(bf16[64,4096]{1,0:T(8,128)(2,1)} %bitcast.64), channel_id=1, source_target_pairs={{0,8},{24,16},{1,9},{25,17},{2,10},{26,18},{3,11},{27,19},{4,12},{... | collective-permute-start | bytes 1572872 | tf_op jit(solution)/shard_map/ppermute | solution.py:291
  43.2 10.7 %cycle.4 = (bf16[4,64,4096]{2,1,0:T(8,128)(2,1)}, bf16[4,64,4096]{2,1,0:T(8,128)(2,1)}) custom-call(s32[32]{0:T(128)} %get-tuple-element.26.slots, s32[32]{0:T(128)} %get-tuple-element.25.blocks, s32[32]{0:T(128)} %bitcast.70, s32[4]{0:T(128)} %iota.3.chunks, bf16[4,128,4096]{2,1,0:T(8,128)(2,1)} %get-tuple-element.14.ladder, ...), custom_call_target="tpu_custom_call" | custom-call | flops 134217728 | bytes 8388608 | tf_op jit(solution)/shard_map/cycle/pallas_call | solution.py:183
  54.0 2.1 %fusion.4 = bf16[64,4096]{1,0:T(8,128)(2,1)} fusion(bf16[64,4096]{1,0:T(8,128)(2,1)S(1)} %collective-permute-done.8, bf16[4,64,4096]{2,1,0:T(8,128)(2,1)} %get-tuple-element.20, s32[]{:T(128)S(6)} %min.19), kind=kLoop, calls=%fused_computation.8 | loop fusion | flops 1048576 | bytes 1572868 | tf_op jit(solution)/shard_map/convert_element_type | solution.py:272
  56.1 1.4 %collective-permute-start.9 = (bf16[64,4096]{1,0:T(8,128)(2,1)}, bf16[64,4096]{1,0:T(8,128)(2,1)}, u32[]{:S(2)}, u32[]{:S(2)}) collective-permute-start(bf16[64,4096]{1,0:T(8,128)(2,1)} %fusion.4), channel_id=1, source_target_pairs={{0,8},{8,16},{1,9},{9,17},{2,10},{10,18},{3,11},{11,19},{4,12},{12... | collective-permute-start | bytes 1572872 | tf_op jit(solution)/shard_map/ppermute | solution.py:294
  57.5 4.0 %collective-permute-start.11 = (bf16[64,4096]{1,0:T(8,128)(2,1)}, bf16[64,4096]{1,0:T(8,128)(2,1)}, u32[]{:S(2)}, u32[]{:S(2)}) collective-permute-start(bf16[64,4096]{1,0:T(8,128)(2,1)} %fusion.4), channel_id=1, source_target_pairs={{24,16},{16,8},{25,17},{17,9},{26,18},{18,10},{27,19},{19,11},{28,... | collective-permute-start | bytes 1572872 | tf_op jit(solution)/shard_map/ppermute | solution.py:295
  61.5 2.2 %fusion = f32[128,4096]{1,0:T(8,128)S(1)} fusion(bf16[128,256]{1,0:T(8,128)(2,1)S(1)} %copy-done, bf16[256,4096]{1,0:T(8,128)(2,1)} %all-gather.2.cloned.1.call-done, bf16[128,1,4096]{2,0,1:T(8,128)(2,1)S(1)} %copy-done.7), kind=kOutput, calls=%fused_computation.1 | convolution fusion | flops 269484032 | bytes 5308416 | tf_op jit(solution)/shard_map/dot_general | solution.py:265
  66.2 4.0 %collective-permute-start.6 = (bf16[64,4096]{1,0:T(8,128)(2,1)S(1)}, bf16[64,4096]{1,0:T(8,128)(2,1)S(1)}, u32[]{:S(2)}, u32[]{:S(2)}) collective-permute-start(bf16[64,4096]{1,0:T(8,128)(2,1)S(1)} %fusion.7), channel_id=1, source_target_pairs={{24,16},{16,8},{25,17},{17,9},{26,18},{18,10},{27,19},{19,11},{28,... | collective-permute-start | bytes 1572872 | tf_op jit(solution)/shard_map/ppermute | solution.py:295
  71.5 2.3 %collective-permute-done.11 = bf16[64,4096]{1,0:T(8,128)(2,1)} collective-permute-done((bf16[64,4096]{1,0:T(8,128)(2,1)}, bf16[64,4096]{1,0:T(8,128)(2,1)}, u32[]{:S(2)}, u32[]{:S(2)}) %collective-permute-start.11) | collective-permute-done | bytes 524320 | tf_op jit(solution)/shard_map/ppermute | solution.py:295
  73.8 1.5 %fusion.5 = (bf16[64,4096]{1,0:T(8,128)(2,1)S(1)}, bf16[64,4096]{1,0:T(8,128)(2,1)S(1)}) fusion(bf16[64,4096]{1,0:T(8,128)(2,1)} %collective-permute-done.9, bf16[4,64,4096]{2,1,0:T(8,128)(2,1)S(1)} %copy-done.6, s32[]{:T(128)S(6)} %min.18, bf16[64,4096]{1,0:T(8,128)(2,1)} %collective-permute-done.11, s32[]{:T(128)S(6)} %min.20), kind=kLoop, calls=%fused_computation.10 | loop fusion | flops 2097152 | bytes 3145736 | tf_op jit(solution)/shard_map/convert_element_type | solution.py:272
  75.3 2.6 %collective-permute-start.12 = (bf16[64,4096]{1,0:T(8,128)(2,1)S(1)}, bf16[64,4096]{1,0:T(8,128)(2,1)S(1)}, u32[]{:S(2)}, u32[]{:S(2)}) collective-permute-start(bf16[64,4096]{1,0:T(8,128)(2,1)S(1)} %get-tuple-element.24), channel_id=1, source_target_pairs={{24,16},{16,8},{8,0},{25,17},{17,9},{9,1},{26,18},{18,10},{10,2},{... | collective-permute-start | bytes 1572872 | tf_op jit(solution)/shard_map/ppermute | solution.py:295
  78.0 2.7 %collective-permute-start.10 = (bf16[64,4096]{1,0:T(8,128)(2,1)S(1)}, bf16[64,4096]{1,0:T(8,128)(2,1)S(1)}, u32[]{:S(2)}, u32[]{:S(2)}) collective-permute-start(bf16[64,4096]{1,0:T(8,128)(2,1)S(1)} %get-tuple-element.23), channel_id=1, source_target_pairs={{0,8},{8,16},{16,24},{1,9},{9,17},{17,25},{2,10},{10,18},{18,26},{... | collective-permute-start | bytes 1572872 | tf_op jit(solution)/shard_map/ppermute | solution.py:294
  80.6 2.0 %collective-permute-done.4 = bf16[64,4096]{1,0:T(8,128)(2,1)S(1)} collective-permute-done((bf16[64,4096]{1,0:T(8,128)(2,1)S(1)}, bf16[64,4096]{1,0:T(8,128)(2,1)S(1)}, u32[]{:S(2)}, u32[]{:S(2)}) %collective-permute-start.4) | collective-permute-done | bytes 524320 | tf_op jit(solution)/shard_map/ppermute | solution.py:294
  82.6 2.3 %collective-permute-done.6 = bf16[64,4096]{1,0:T(8,128)(2,1)S(1)} collective-permute-done((bf16[64,4096]{1,0:T(8,128)(2,1)S(1)}, bf16[64,4096]{1,0:T(8,128)(2,1)S(1)}, u32[]{:S(2)}, u32[]{:S(2)}) %collective-permute-start.6) | collective-permute-done | bytes 524320 | tf_op jit(solution)/shard_map/ppermute | solution.py:295
  85.2 2.6 %collective-permute-start.7 = (bf16[64,4096]{1,0:T(8,128)(2,1)S(1)}, bf16[64,4096]{1,0:T(8,128)(2,1)S(1)}, u32[]{:S(2)}, u32[]{:S(2)}) collective-permute-start(bf16[64,4096]{1,0:T(8,128)(2,1)S(1)} %get-tuple-element.22), channel_id=1, source_target_pairs={{24,16},{16,8},{8,0},{25,17},{17,9},{9,1},{26,18},{18,10},{10,2},{... | collective-permute-start | bytes 1572872 | tf_op jit(solution)/shard_map/ppermute | solution.py:295
  87.9 2.7 %collective-permute-start.5 = (bf16[64,4096]{1,0:T(8,128)(2,1)S(1)}, bf16[64,4096]{1,0:T(8,128)(2,1)S(1)}, u32[]{:S(2)}, u32[]{:S(2)}) collective-permute-start(bf16[64,4096]{1,0:T(8,128)(2,1)S(1)} %get-tuple-element.21), channel_id=1, source_target_pairs={{0,8},{8,16},{16,24},{1,9},{9,17},{17,25},{2,10},{10,18},{18,26},{... | collective-permute-start | bytes 1572872 | tf_op jit(solution)/shard_map/ppermute | solution.py:294
  90.6 5.6 %collective-permute-done.12 = bf16[64,4096]{1,0:T(8,128)(2,1)S(1)} collective-permute-done((bf16[64,4096]{1,0:T(8,128)(2,1)S(1)}, bf16[64,4096]{1,0:T(8,128)(2,1)S(1)}, u32[]{:S(2)}, u32[]{:S(2)}) %collective-permute-start.12) | collective-permute-done | bytes 524320 | tf_op jit(solution)/shard_map/ppermute | solution.py:295
  96.4 11.1 %collective-permute-done.7 = bf16[64,4096]{1,0:T(8,128)(2,1)S(1)} collective-permute-done((bf16[64,4096]{1,0:T(8,128)(2,1)S(1)}, bf16[64,4096]{1,0:T(8,128)(2,1)S(1)}, u32[]{:S(2)}, u32[]{:S(2)}) %collective-permute-start.7) | collective-permute-done | bytes 524320 | tf_op jit(solution)/shard_map/ppermute | solution.py:295
  107.6 1.5 %fusion.9 = bf16[128,1,4096]{2,0,1:T(8,128)(2,1)} fusion(s32[4096]{0:T(1024)S(1)} %bitcast.67, s32[128]{0:T(128)S(1)} %copy-done.10, f32[128,4096]{1,0:T(8,128)S(1)} %fusion, f32[64,4096]{1,0:T(8,128)S(1)} %convert_add_fusion.3, f32[64,4096]{1,0:T(8,128)S(1)} %convert_add_fusion.7), kind=kLoop, calls=%fused_computation.19 | loop fusion | flops 3670016 | bytes 5259776 | tf_op jit(solution)/shard_map/reshape | solution.py:307
  (42 shorter events, 9.2 us)
Async XLA Ops:
  6.5 55.0 %copy-start = (bf16[128,256]{1,0:T(8,128)(2,1)S(1)}, bf16[128,256]{1,0:T(8,128)(2,1)}, u32[]{:S(2)}) copy-start(bf16[128,256]{1,0:T(8,128)(2,1)} %param.13) | copy-start | bytes 196612
  6.5 55.0 %all-gather.2.cloned.1.call-start = ((), (), s32[]{:S(2)}) async-start(), calls=%async_computation | async-start | bytes 3145728 | tf_op jit(solution)/shard_map/all_gather | solution.py:242
  7.7 17.6 %copy-start.1 = (bf16[128,2048]{1,0:T(8,128)(2,1)}, bf16[128,2048]{1,0:T(8,128)(2,1)S(1)}, u32[]{:S(2)}) copy-start(bf16[128,2048]{1,0:T(8,128)(2,1)S(1)} %slice.4.rest_0_) | copy-start | bytes 1572868
  7.7 19.1 %collective-permute-start = (bf16[128,2048]{1,0:T(8,128)(2,1)S(1)}, bf16[128,2048]{1,0:T(8,128)(2,1)S(1)}, u32[]{:S(2)}, u32[]{:S(2)}) collective-permute-start(bf16[128,2048]{1,0:T(8,128)(2,1)S(1)} %slice.4.rest_0_), channel_id=1, source_target_pairs={{0,2},{1,3},{2,0},{3,1},{4,6},{5,7},{6,4},{7,5},{8,10},{9,11},{10,... | collective-permute-start | bytes 1572872 | tf_op jit(solution)/shard_map/ppermute | solution.py:249
  9.6 17.2 %copy-start.9 = (s32[32,1]{0,1:T(1,128)S(1)}, s32[32,1]{0,1:T(1,128)}, u32[]{:S(2)}) copy-start(s32[32,1]{0,1:T(1,128)} %param.20) | copy-start | bytes 388
  25.2 3.0 %collective-permute-start.1 = (bf16[128,2048]{1,0:T(8,128)(2,1)S(1)}, bf16[128,2048]{1,0:T(8,128)(2,1)S(1)}, u32[]{:S(2)}, u32[]{:S(2)}) collective-permute-start(bf16[128,2048]{1,0:T(8,128)(2,1)S(1)} %slice.4.rest_0_), channel_id=1, source_target_pairs={{0,1},{1,0},{2,3},{3,2},{4,5},{5,4},{6,7},{7,6},{8,9},{9,8},{10,11... | collective-permute-start | bytes 1572872 | tf_op jit(solution)/shard_map/ppermute | solution.py:249
  26.7 2.3 %copy-start.2 = (bf16[128,2048]{1,0:T(8,128)(2,1)}, bf16[128,2048]{1,0:T(8,128)(2,1)S(1)}, u32[]{:S(2)}) copy-start(bf16[128,2048]{1,0:T(8,128)(2,1)S(1)} %collective-permute-done.rest_2_) | copy-start | bytes 1572868
  26.7 2.3 %collective-permute-start.2 = (bf16[128,2048]{1,0:T(8,128)(2,1)S(1)}, bf16[128,2048]{1,0:T(8,128)(2,1)S(1)}, u32[]{:S(2)}, u32[]{:S(2)}) collective-permute-start(bf16[128,2048]{1,0:T(8,128)(2,1)S(1)} %collective-permute-done.rest_2_), channel_id=1, source_target_pairs={{0,1},{1,0},{2,3},{3,2},{4,5},{5,4},{6,7},{7,6},{8,9},{9,8},{10,11... | collective-permute-start | bytes 1572872 | tf_op jit(solution)/shard_map/ppermute | solution.py:249
  29.0 0.8 copy-start.4
  35.1 18.9 %collective-permute-start.8 = (bf16[64,4096]{1,0:T(8,128)(2,1)}, bf16[64,4096]{1,0:T(8,128)(2,1)S(1)}, u32[]{:S(2)}, u32[]{:S(2)}) collective-permute-start(bf16[64,4096]{1,0:T(8,128)(2,1)} %bitcast.63), channel_id=1, source_target_pairs={{0,8},{24,16},{1,9},{25,17},{2,10},{26,18},{3,11},{27,19},{4,12},{... | collective-permute-start | bytes 1572872 | tf_op jit(solution)/shard_map/ppermute | solution.py:291
  41.4 22.3 %collective-permute-start.3 = (bf16[64,4096]{1,0:T(8,128)(2,1)}, bf16[64,4096]{1,0:T(8,128)(2,1)}, u32[]{:S(2)}, u32[]{:S(2)}) collective-permute-start(bf16[64,4096]{1,0:T(8,128)(2,1)} %bitcast.64), channel_id=1, source_target_pairs={{0,8},{24,16},{1,9},{25,17},{2,10},{26,18},{3,11},{27,19},{4,12},{... | collective-permute-start | bytes 1572872 | tf_op jit(solution)/shard_map/ppermute | solution.py:291
  54.0 7.6 %copy-start.7 = (bf16[128,1,4096]{2,0,1:T(8,128)(2,1)S(1)}, bf16[128,1,4096]{2,0,1:T(8,128)(2,1)}, u32[]{:S(2)}) copy-start(bf16[128,1,4096]{2,0,1:T(8,128)(2,1)} %param.14) | copy-start | bytes 3145732
  56.1 7.7 %copy-start.5 = (bf16[4,64,4096]{2,1,0:T(8,128)(2,1)S(1)}, bf16[4,64,4096]{2,1,0:T(8,128)(2,1)}, u32[]{:S(2)}) copy-start(bf16[4,64,4096]{2,1,0:T(8,128)(2,1)} %get-tuple-element.18) | copy-start | bytes 6291460
  56.1 15.4 %collective-permute-start.9 = (bf16[64,4096]{1,0:T(8,128)(2,1)}, bf16[64,4096]{1,0:T(8,128)(2,1)}, u32[]{:S(2)}, u32[]{:S(2)}) collective-permute-start(bf16[64,4096]{1,0:T(8,128)(2,1)} %fusion.4), channel_id=1, source_target_pairs={{0,8},{8,16},{1,9},{9,17},{2,10},{10,18},{3,11},{11,19},{4,12},{12... | collective-permute-start | bytes 1572872 | tf_op jit(solution)/shard_map/ppermute | solution.py:294
  57.5 16.3 %collective-permute-start.11 = (bf16[64,4096]{1,0:T(8,128)(2,1)}, bf16[64,4096]{1,0:T(8,128)(2,1)}, u32[]{:S(2)}, u32[]{:S(2)}) collective-permute-start(bf16[64,4096]{1,0:T(8,128)(2,1)} %fusion.4), channel_id=1, source_target_pairs={{24,16},{16,8},{25,17},{17,9},{26,18},{18,10},{27,19},{19,11},{28,... | collective-permute-start | bytes 1572872 | tf_op jit(solution)/shard_map/ppermute | solution.py:295
  61.5 12.3 %copy-start.6 = (bf16[4,64,4096]{2,1,0:T(8,128)(2,1)S(1)}, bf16[4,64,4096]{2,1,0:T(8,128)(2,1)}, u32[]{:S(2)}) copy-start(bf16[4,64,4096]{2,1,0:T(8,128)(2,1)} %get-tuple-element.20) | copy-start | bytes 6291460
  64.9 17.7 %collective-permute-start.4 = (bf16[64,4096]{1,0:T(8,128)(2,1)S(1)}, bf16[64,4096]{1,0:T(8,128)(2,1)S(1)}, u32[]{:S(2)}, u32[]{:S(2)}) collective-permute-start(bf16[64,4096]{1,0:T(8,128)(2,1)S(1)} %fusion.7), channel_id=1, source_target_pairs={{0,8},{8,16},{1,9},{9,17},{2,10},{10,18},{3,11},{11,19},{4,12},{12... | collective-permute-start | bytes 1572872 | tf_op jit(solution)/shard_map/ppermute | solution.py:294
  66.2 18.7 %collective-permute-start.6 = (bf16[64,4096]{1,0:T(8,128)(2,1)S(1)}, bf16[64,4096]{1,0:T(8,128)(2,1)S(1)}, u32[]{:S(2)}, u32[]{:S(2)}) collective-permute-start(bf16[64,4096]{1,0:T(8,128)(2,1)S(1)} %fusion.7), channel_id=1, source_target_pairs={{24,16},{16,8},{25,17},{17,9},{26,18},{18,10},{27,19},{19,11},{28,... | collective-permute-start | bytes 1572872 | tf_op jit(solution)/shard_map/ppermute | solution.py:295
  75.3 20.9 %collective-permute-start.12 = (bf16[64,4096]{1,0:T(8,128)(2,1)S(1)}, bf16[64,4096]{1,0:T(8,128)(2,1)S(1)}, u32[]{:S(2)}, u32[]{:S(2)}) collective-permute-start(bf16[64,4096]{1,0:T(8,128)(2,1)S(1)} %get-tuple-element.24), channel_id=1, source_target_pairs={{24,16},{16,8},{8,0},{25,17},{17,9},{9,1},{26,18},{18,10},{10,2},{... | collective-permute-start | bytes 1572872 | tf_op jit(solution)/shard_map/ppermute | solution.py:295
  78.0 18.2 %collective-permute-start.10 = (bf16[64,4096]{1,0:T(8,128)(2,1)S(1)}, bf16[64,4096]{1,0:T(8,128)(2,1)S(1)}, u32[]{:S(2)}, u32[]{:S(2)}) collective-permute-start(bf16[64,4096]{1,0:T(8,128)(2,1)S(1)} %get-tuple-element.23), channel_id=1, source_target_pairs={{0,8},{8,16},{16,24},{1,9},{9,17},{17,25},{2,10},{10,18},{18,26},{... | collective-permute-start | bytes 1572872 | tf_op jit(solution)/shard_map/ppermute | solution.py:294
  85.2 22.2 %collective-permute-start.7 = (bf16[64,4096]{1,0:T(8,128)(2,1)S(1)}, bf16[64,4096]{1,0:T(8,128)(2,1)S(1)}, u32[]{:S(2)}, u32[]{:S(2)}) collective-permute-start(bf16[64,4096]{1,0:T(8,128)(2,1)S(1)} %get-tuple-element.22), channel_id=1, source_target_pairs={{24,16},{16,8},{8,0},{25,17},{17,9},{9,1},{26,18},{18,10},{10,2},{... | collective-permute-start | bytes 1572872 | tf_op jit(solution)/shard_map/ppermute | solution.py:295
  87.9 19.7 %copy-start.8 = (s32[1,4096]{1,0:T(1,128)S(1)}, s32[1,4096]{1,0:T(1,128)}, u32[]{:S(2)}) copy-start(s32[1,4096]{1,0:T(1,128)} %param.23) | copy-start | bytes 49156
  87.9 19.7 %copy-start.10 = (s32[128]{0:T(128)S(1)}, s32[128]{0:T(128)}, u32[]{:S(2)}) copy-start(s32[128]{0:T(128)} %param.22) | copy-start | bytes 1540
  87.9 19.5 %collective-permute-start.5 = (bf16[64,4096]{1,0:T(8,128)(2,1)S(1)}, bf16[64,4096]{1,0:T(8,128)(2,1)S(1)}, u32[]{:S(2)}, u32[]{:S(2)}) collective-permute-start(bf16[64,4096]{1,0:T(8,128)(2,1)S(1)} %get-tuple-element.21), channel_id=1, source_target_pairs={{0,8},{8,16},{16,24},{1,9},{9,17},{17,25},{2,10},{10,18},{18,26},{... | collective-permute-start | bytes 1572872 | tf_op jit(solution)/shard_map/ppermute | solution.py:294
  (1 other events, 0.8 us)
Sparse Core Ops, SparseCore 0:
  25.3 33.4 all-gather.1

commit v5 on v4

--- a/solution.py
+++ b/solution.py
@@ -259,7 +259,7 @@
 
     finish = functools.partial(add_cycle, ladder, cycle_tiles, pieces, slots, blocks, targets)
     edge = jnp.where(z == 0, n - 1, 0).astype(jnp.int32)
-    first_shares = [finish(edge[None], part=p)[0] for p in range(PIECES)]
+    first_shares = finish(edge[None])
     shares = finish(jnp.arange(n, dtype=jnp.int32))
 
     hole = jnp.dot(hole_ladder, owned_all, preferred_element_type=jnp.float32)

time: 118 us -> 116 us (0.983)
  the two profiles are of different devices: /device:TPU:17 before, /device:TPU:22 now
where the time goes in v5:
time: 116 us; the launch traced here: 115 us
  starting transfers between devices  31.6 us (27%)
  waiting for transfers between devices  30.2 us (26%)
  Pallas kernels  26.9 us (23%)
  between operations  14.3 us (12%)
  other arithmetic  7.39 us (6%)
  local copies, waits for them, and re-layouts  2.54 us (2%)
  matrix products  2.19 us (2%)
    ppermute x4, waiting for transfers between devices, per_device(): lax.ppermute(down, 'sec', down_pairs)  23.5 us
    pallas_call x2, Pallas kernels, add_cycle(): pl.pallas_call(functools.partial(cycle_kernel, part, outputs), grid_spec=...  16.7 us
    ppermute x4, starting transfers between devices, per_device(): lax.ppermute(down, 'sec', down_pairs)  13.3 us
    ppermute x4, starting transfers between devices, per_device(): lax.ppermute(up, 'sec', up_pairs)  10.2 us
    pallas_call x1, Pallas kernels, ladder_term(): pl.pallas_call(ladder_kernel, grid_spec=pltpu.PrefetchScalarGridSpec(num_...  10.2 us
    ppermute x3, starting transfers between devices, per_device(): held[j ^ bit] = lax.ppermute(held[j], 'inner', pairs)  5.43 us
    ppermute x2, waiting for transfers between devices, per_device(): going[p] = [lax.ppermute(up, 'sec', up_pairs + down_pairs)]  5.04 us
    convert_element_type x4, other arithmetic, plus(): return (a.astype(jnp.float32) + b.astype(jnp.float32)).astype(jnp.bfloat16)  4.86 us
  transfers between devices with their start and end apart: 14, of which 10 were waited for; matrix products, arithmetic and copies ran while one was open for 7% of the time, Pallas kernels for 23%

profile of v5, /device:TPU:22, one launch (start us, length us, event | category | flops | bytes accessed | tf_op | source)
XLA Modules:
  0.0 115.1 jit_solution(4096630682893094632)
XLA Ops:
  8.9 10.2 %ladder.1 = (bf16[4,128,4096]{2,1,0:T(8,128)(2,1)}, bf16[128,4096]{1,0:T(8,128)(2,1)}) custom-call(s32[256]{0:T(256)} %bitcast.70, s32[256]{0:T(256)} %bitcast.71, s32[1]{0:T(128)} %bitcast.62.live, s32[1]{0:T(128)} %bitcast.7.place, bf16[128,16384]{1,0:T(8,128)(2,1)} %bitcast.64, bf16[256,128,128]{2,1,0:T(8,128)(2,1)} %tiles.1), custom_call_target="tpu_custom_call" | custom-call | flops 4294967296 | bytes 41943040 | tf_op jit(solution)/shard_map/ladder/pallas_call | solution.py:84
  19.2 4.8 %collective-permute-start.1 = (bf16[128,2048]{1,0:T(8,128)(2,1)S(1)}, bf16[128,2048]{1,0:T(8,128)(2,1)S(1)}, u32[]{:S(2)}, u32[]{:S(2)}) collective-permute-start(bf16[128,2048]{1,0:T(8,128)(2,1)S(1)} %slice.4.rest_0_), channel_id=1, source_target_pairs={{0,1},{1,0},{2,3},{3,2},{4,5},{5,4},{6,7},{7,6},{8,9},{9,8},{10,11... | collective-permute-start | bytes 1572872 | tf_op jit(solution)/shard_map/ppermute | solution.py:249
  27.0 6.0 %cycle.2 = (bf16[1,64,4096]{2,1,0:T(8,128)(2,1)}, bf16[1,64,4096]{2,1,0:T(8,128)(2,1)}) custom-call(s32[32]{0:T(128)} %get-tuple-element.30.slots, s32[32]{0:T(128)} %get-tuple-element.29.blocks, s32[32]{0:T(128)} %bitcast.66, s32[1]{0:T(128)} %bitcast.2.chunks, bf16[4,128,4096]{2,1,0:T(8,128)(2,1)} %get-tuple-element.16.ladder, ...), custom_call_target="tpu_custom_call" | custom-call | flops 134217728 | bytes 8388608 | tf_op jit(solution)/shard_map/cycle/pallas_call | solution.py:183
  33.0 1.3 %collective-permute-start.8 = (bf16[64,4096]{1,0:T(8,128)(2,1)}, bf16[64,4096]{1,0:T(8,128)(2,1)S(1)}, u32[]{:S(2)}, u32[]{:S(2)}) collective-permute-start(bf16[64,4096]{1,0:T(8,128)(2,1)} %bitcast.69), channel_id=1, source_target_pairs={{0,8},{24,16},{1,9},{25,17},{2,10},{26,18},{3,11},{27,19},{4,12},{... | collective-permute-start | bytes 1572872 | tf_op jit(solution)/shard_map/ppermute | solution.py:291
  34.3 1.3 %collective-permute-start.3 = (bf16[64,4096]{1,0:T(8,128)(2,1)}, bf16[64,4096]{1,0:T(8,128)(2,1)}, u32[]{:S(2)}, u32[]{:S(2)}) collective-permute-start(bf16[64,4096]{1,0:T(8,128)(2,1)} %bitcast.68), channel_id=1, source_target_pairs={{0,8},{24,16},{1,9},{25,17},{2,10},{26,18},{3,11},{27,19},{4,12},{... | collective-permute-start | bytes 1572872 | tf_op jit(solution)/shard_map/ppermute | solution.py:291
  36.2 10.7 %cycle.3 = (bf16[4,64,4096]{2,1,0:T(8,128)(2,1)}, bf16[4,64,4096]{2,1,0:T(8,128)(2,1)}) custom-call(s32[32]{0:T(128)} %get-tuple-element.30.slots, s32[32]{0:T(128)} %get-tuple-element.29.blocks, s32[32]{0:T(128)} %bitcast.67, s32[4]{0:T(128)} %iota.3.chunks, bf16[4,128,4096]{2,1,0:T(8,128)(2,1)} %get-tuple-element.16.ladder, ...), custom_call_target="tpu_custom_call" | custom-call | flops 134217728 | bytes 8388608 | tf_op jit(solution)/shard_map/cycle/pallas_call | solution.py:183
  47.0 3.9 %collective-permute-done.8 = bf16[64,4096]{1,0:T(8,128)(2,1)S(1)} collective-permute-done((bf16[64,4096]{1,0:T(8,128)(2,1)}, bf16[64,4096]{1,0:T(8,128)(2,1)S(1)}, u32[]{:S(2)}, u32[]{:S(2)}) %collective-permute-start.8) | collective-permute-done | bytes 524320 | tf_op jit(solution)/shard_map/ppermute | solution.py:291
  50.9 2.0 %fusion.4 = bf16[64,4096]{1,0:T(8,128)(2,1)} fusion(bf16[64,4096]{1,0:T(8,128)(2,1)S(1)} %collective-permute-done.8, bf16[4,64,4096]{2,1,0:T(8,128)(2,1)} %get-tuple-element.23, s32[]{:T(128)S(6)} %min.19), kind=kLoop, calls=%fused_computation.8 | loop fusion | flops 1048576 | bytes 1572868 | tf_op jit(solution)/shard_map/convert_element_type | solution.py:272
  52.9 1.4 %collective-permute-start.9 = (bf16[64,4096]{1,0:T(8,128)(2,1)}, bf16[64,4096]{1,0:T(8,128)(2,1)}, u32[]{:S(2)}, u32[]{:S(2)}) collective-permute-start(bf16[64,4096]{1,0:T(8,128)(2,1)} %fusion.4), channel_id=1, source_target_pairs={{0,8},{8,16},{1,9},{9,17},{2,10},{10,18},{3,11},{11,19},{4,12},{12... | collective-permute-start | bytes 1572872 | tf_op jit(solution)/shard_map/ppermute | solution.py:294
  54.3 4.6 %collective-permute-start.11 = (bf16[64,4096]{1,0:T(8,128)(2,1)}, bf16[64,4096]{1,0:T(8,128)(2,1)}, u32[]{:S(2)}, u32[]{:S(2)}) collective-permute-start(bf16[64,4096]{1,0:T(8,128)(2,1)} %fusion.4), channel_id=1, source_target_pairs={{24,16},{16,8},{25,17},{17,9},{26,18},{18,10},{27,19},{19,11},{28,... | collective-permute-start | bytes 1572872 | tf_op jit(solution)/shard_map/ppermute | solution.py:295
  58.9 2.2 %fusion = f32[128,4096]{1,0:T(8,128)S(1)} fusion(bf16[128,256]{1,0:T(8,128)(2,1)S(1)} %copy-done, bf16[256,4096]{1,0:T(8,128)(2,1)} %all-gather.2.cloned.1.call-done, bf16[128,1,4096]{2,0,1:T(8,128)(2,1)S(1)} %copy-done.7), kind=kOutput, calls=%fused_computation.1 | convolution fusion | flops 269484032 | bytes 5308416 | tf_op jit(solution)/shard_map/dot_general | solution.py:265
  62.2 1.2 %fusion.7 = bf16[64,4096]{1,0:T(8,128)(2,1)S(1)} fusion(bf16[64,4096]{1,0:T(8,128)(2,1)} %collective-permute-done.3, bf16[4,64,4096]{2,1,0:T(8,128)(2,1)S(1)} %copy-done.2, s32[]{:T(128)S(6)} %min.19), kind=kLoop, calls=%fused_computation.15 | loop fusion | flops 1048576 | bytes 1572868 | tf_op jit(solution)/shard_map/convert_element_type | solution.py:272
  63.4 1.3 %collective-permute-start.4 = (bf16[64,4096]{1,0:T(8,128)(2,1)S(1)}, bf16[64,4096]{1,0:T(8,128)(2,1)S(1)}, u32[]{:S(2)}, u32[]{:S(2)}) collective-permute-start(bf16[64,4096]{1,0:T(8,128)(2,1)S(1)} %fusion.7), channel_id=1, source_target_pairs={{0,8},{8,16},{1,9},{9,17},{2,10},{10,18},{3,11},{11,19},{4,12},{12... | collective-permute-start | bytes 1572872 | tf_op jit(solution)/shard_map/ppermute | solution.py:294
  64.7 4.6 %collective-permute-start.6 = (bf16[64,4096]{1,0:T(8,128)(2,1)S(1)}, bf16[64,4096]{1,0:T(8,128)(2,1)S(1)}, u32[]{:S(2)}, u32[]{:S(2)}) collective-permute-start(bf16[64,4096]{1,0:T(8,128)(2,1)S(1)} %fusion.7), channel_id=1, source_target_pairs={{24,16},{16,8},{25,17},{17,9},{26,18},{18,10},{27,19},{19,11},{28,... | collective-permute-start | bytes 1572872 | tf_op jit(solution)/shard_map/ppermute | solution.py:295
  69.3 4.2 %collective-permute-done.11 = bf16[64,4096]{1,0:T(8,128)(2,1)} collective-permute-done((bf16[64,4096]{1,0:T(8,128)(2,1)}, bf16[64,4096]{1,0:T(8,128)(2,1)}, u32[]{:S(2)}, u32[]{:S(2)}) %collective-permute-start.11) | collective-permute-done | bytes 524320 | tf_op jit(solution)/shard_map/ppermute | solution.py:295
  73.5 1.5 %fusion.5 = (bf16[64,4096]{1,0:T(8,128)(2,1)S(1)}, bf16[64,4096]{1,0:T(8,128)(2,1)S(1)}) fusion(bf16[64,4096]{1,0:T(8,128)(2,1)} %collective-permute-done.9, bf16[4,64,4096]{2,1,0:T(8,128)(2,1)S(1)} %copy-done.3, s32[]{:T(128)S(6)} %min.18, bf16[64,4096]{1,0:T(8,128)(2,1)} %collective-permute-done.11, s32[]{:T(128)S(6)} %min.20), kind=kLoop, calls=%fused_computation.10 | loop fusion | flops 2097152 | bytes 3145736 | tf_op jit(solution)/shard_map/convert_element_type | solution.py:272
  74.9 2.1 %collective-permute-start.12 = (bf16[64,4096]{1,0:T(8,128)(2,1)S(1)}, bf16[64,4096]{1,0:T(8,128)(2,1)S(1)}, u32[]{:S(2)}, u32[]{:S(2)}) collective-permute-start(bf16[64,4096]{1,0:T(8,128)(2,1)S(1)} %get-tuple-element.28), channel_id=1, source_target_pairs={{24,16},{16,8},{8,0},{25,17},{17,9},{9,1},{26,18},{18,10},{10,2},{... | collective-permute-start | bytes 1572872 | tf_op jit(solution)/shard_map/ppermute | solution.py:295
  77.0 3.8 %collective-permute-start.10 = (bf16[64,4096]{1,0:T(8,128)(2,1)S(1)}, bf16[64,4096]{1,0:T(8,128)(2,1)S(1)}, u32[]{:S(2)}, u32[]{:S(2)}) collective-permute-start(bf16[64,4096]{1,0:T(8,128)(2,1)S(1)} %get-tuple-element.27), channel_id=1, source_target_pairs={{0,8},{8,16},{16,24},{1,9},{9,17},{17,25},{2,10},{10,18},{18,26},{... | collective-permute-start | bytes 1572872 | tf_op jit(solution)/shard_map/ppermute | solution.py:294
  80.8 3.8 %collective-permute-done.6 = bf16[64,4096]{1,0:T(8,128)(2,1)S(1)} collective-permute-done((bf16[64,4096]{1,0:T(8,128)(2,1)S(1)}, bf16[64,4096]{1,0:T(8,128)(2,1)S(1)}, u32[]{:S(2)}, u32[]{:S(2)}) %collective-permute-start.6) | collective-permute-done | bytes 524320 | tf_op jit(solution)/shard_map/ppermute | solution.py:295
  84.9 2.1 %collective-permute-start.7 = (bf16[64,4096]{1,0:T(8,128)(2,1)S(1)}, bf16[64,4096]{1,0:T(8,128)(2,1)S(1)}, u32[]{:S(2)}, u32[]{:S(2)}) collective-permute-start(bf16[64,4096]{1,0:T(8,128)(2,1)S(1)} %get-tuple-element.26), channel_id=1, source_target_pairs={{24,16},{16,8},{8,0},{25,17},{17,9},{9,1},{26,18},{18,10},{10,2},{... | collective-permute-start | bytes 1572872 | tf_op jit(solution)/shard_map/ppermute | solution.py:295
  87.0 3.8 %collective-permute-start.5 = (bf16[64,4096]{1,0:T(8,128)(2,1)S(1)}, bf16[64,4096]{1,0:T(8,128)(2,1)S(1)}, u32[]{:S(2)}, u32[]{:S(2)}) collective-permute-start(bf16[64,4096]{1,0:T(8,128)(2,1)S(1)} %get-tuple-element.25), channel_id=1, source_target_pairs={{0,8},{8,16},{16,24},{1,9},{9,17},{17,25},{2,10},{10,18},{18,26},{... | collective-permute-start | bytes 1572872 | tf_op jit(solution)/shard_map/ppermute | solution.py:294
  90.8 5.1 %collective-permute-done.12 = bf16[64,4096]{1,0:T(8,128)(2,1)S(1)} collective-permute-done((bf16[64,4096]{1,0:T(8,128)(2,1)S(1)}, bf16[64,4096]{1,0:T(8,128)(2,1)S(1)}, u32[]{:S(2)}, u32[]{:S(2)}) %collective-permute-start.12) | collective-permute-done | bytes 524320 | tf_op jit(solution)/shard_map/ppermute | solution.py:295
  96.0 10.5 %collective-permute-done.7 = bf16[64,4096]{1,0:T(8,128)(2,1)S(1)} collective-permute-done((bf16[64,4096]{1,0:T(8,128)(2,1)S(1)}, bf16[64,4096]{1,0:T(8,128)(2,1)S(1)}, u32[]{:S(2)}, u32[]{:S(2)}) %collective-permute-start.7) | collective-permute-done | bytes 524320 | tf_op jit(solution)/shard_map/ppermute | solution.py:295
  106.8 1.5 %fusion.9 = bf16[128,1,4096]{2,0,1:T(8,128)(2,1)} fusion(s32[4096]{0:T(1024)S(1)} %bitcast.65, s32[128]{0:T(128)S(1)} %copy-done.10, f32[128,4096]{1,0:T(8,128)S(1)} %fusion, f32[64,4096]{1,0:T(8,128)S(1)} %convert_add_fusion.3, f32[64,4096]{1,0:T(8,128)S(1)} %convert_add_fusion.7), kind=kLoop, calls=%fused_computation.19 | loop fusion | flops 3670016 | bytes 5259776 | tf_op jit(solution)/shard_map/reshape | solution.py:307
  (41 shorter events, 7.3 us)
Async XLA Ops:
  6.5 52.4 %copy-start = (bf16[128,256]{1,0:T(8,128)(2,1)S(1)}, bf16[128,256]{1,0:T(8,128)(2,1)}, u32[]{:S(2)}) copy-start(bf16[128,256]{1,0:T(8,128)(2,1)} %param.13) | copy-start | bytes 196612
  6.5 52.4 %all-gather.2.cloned.1.call-start = ((), (), s32[]{:S(2)}) async-start(), calls=%async_computation | async-start | bytes 3145728 | tf_op jit(solution)/shard_map/all_gather | solution.py:242
  7.7 11.5 %copy-start.1 = (bf16[128,2048]{1,0:T(8,128)(2,1)}, bf16[128,2048]{1,0:T(8,128)(2,1)S(1)}, u32[]{:S(2)}) copy-start(bf16[128,2048]{1,0:T(8,128)(2,1)S(1)} %slice.4.rest_0_) | copy-start | bytes 1572868
  7.7 16.3 %collective-permute-start = (bf16[128,2048]{1,0:T(8,128)(2,1)S(1)}, bf16[128,2048]{1,0:T(8,128)(2,1)S(1)}, u32[]{:S(2)}, u32[]{:S(2)}) collective-permute-start(bf16[128,2048]{1,0:T(8,128)(2,1)S(1)} %slice.4.rest_0_), channel_id=1, source_target_pairs={{0,2},{1,3},{2,0},{3,1},{4,6},{5,7},{6,4},{7,5},{8,10},{9,11},{10,... | collective-permute-start | bytes 1572872 | tf_op jit(solution)/shard_map/ppermute | solution.py:249
  8.9 15.1 %copy-start.9 = (s32[32,1]{0,1:T(1,128)S(1)}, s32[32,1]{0,1:T(1,128)}, u32[]{:S(2)}) copy-start(s32[32,1]{0,1:T(1,128)} %param.20) | copy-start | bytes 388
  19.2 6.3 %collective-permute-start.1 = (bf16[128,2048]{1,0:T(8,128)(2,1)S(1)}, bf16[128,2048]{1,0:T(8,128)(2,1)S(1)}, u32[]{:S(2)}, u32[]{:S(2)}) collective-permute-start(bf16[128,2048]{1,0:T(8,128)(2,1)S(1)} %slice.4.rest_0_), channel_id=1, source_target_pairs={{0,1},{1,0},{2,3},{3,2},{4,5},{5,4},{6,7},{7,6},{8,9},{9,8},{10,11... | collective-permute-start | bytes 1572872 | tf_op jit(solution)/shard_map/ppermute | solution.py:249
  23.9 2.3 %copy-start.4 = (bf16[128,2048]{1,0:T(8,128)(2,1)}, bf16[128,2048]{1,0:T(8,128)(2,1)S(1)}, u32[]{:S(2)}) copy-start(bf16[128,2048]{1,0:T(8,128)(2,1)S(1)} %collective-permute-done.rest_2_) | copy-start | bytes 1572868
  23.9 2.3 %collective-permute-start.2 = (bf16[128,2048]{1,0:T(8,128)(2,1)S(1)}, bf16[128,2048]{1,0:T(8,128)(2,1)S(1)}, u32[]{:S(2)}, u32[]{:S(2)}) collective-permute-start(bf16[128,2048]{1,0:T(8,128)(2,1)S(1)} %collective-permute-done.rest_2_), channel_id=1, source_target_pairs={{0,1},{1,0},{2,3},{3,2},{4,5},{5,4},{6,7},{7,6},{8,9},{9,8},{10,11... | collective-permute-start | bytes 1572872 | tf_op jit(solution)/shard_map/ppermute | solution.py:249
  26.2 0.8 copy-start.6
  33.0 17.9 %collective-permute-start.8 = (bf16[64,4096]{1,0:T(8,128)(2,1)}, bf16[64,4096]{1,0:T(8,128)(2,1)S(1)}, u32[]{:S(2)}, u32[]{:S(2)}) collective-permute-start(bf16[64,4096]{1,0:T(8,128)(2,1)} %bitcast.69), channel_id=1, source_target_pairs={{0,8},{24,16},{1,9},{25,17},{2,10},{26,18},{3,11},{27,19},{4,12},{... | collective-permute-start | bytes 1572872 | tf_op jit(solution)/shard_map/ppermute | solution.py:291
  34.3 27.9 %collective-permute-start.3 = (bf16[64,4096]{1,0:T(8,128)(2,1)}, bf16[64,4096]{1,0:T(8,128)(2,1)}, u32[]{:S(2)}, u32[]{:S(2)}) collective-permute-start(bf16[64,4096]{1,0:T(8,128)(2,1)} %bitcast.68), channel_id=1, source_target_pairs={{0,8},{24,16},{1,9},{25,17},{2,10},{26,18},{3,11},{27,19},{4,12},{... | collective-permute-start | bytes 1572872 | tf_op jit(solution)/shard_map/ppermute | solution.py:291
  46.9 12.0 %copy-start.7 = (bf16[128,1,4096]{2,0,1:T(8,128)(2,1)S(1)}, bf16[128,1,4096]{2,0,1:T(8,128)(2,1)}, u32[]{:S(2)}) copy-start(bf16[128,1,4096]{2,0,1:T(8,128)(2,1)} %param.14) | copy-start | bytes 3145732
  52.9 9.4 %copy-start.2 = (bf16[4,64,4096]{2,1,0:T(8,128)(2,1)S(1)}, bf16[4,64,4096]{2,1,0:T(8,128)(2,1)}, u32[]{:S(2)}) copy-start(bf16[4,64,4096]{2,1,0:T(8,128)(2,1)} %get-tuple-element.21) | copy-start | bytes 6291460
  52.9 16.4 %collective-permute-start.9 = (bf16[64,4096]{1,0:T(8,128)(2,1)}, bf16[64,4096]{1,0:T(8,128)(2,1)}, u32[]{:S(2)}, u32[]{:S(2)}) collective-permute-start(bf16[64,4096]{1,0:T(8,128)(2,1)} %fusion.4), channel_id=1, source_target_pairs={{0,8},{8,16},{1,9},{9,17},{2,10},{10,18},{3,11},{11,19},{4,12},{12... | collective-permute-start | bytes 1572872 | tf_op jit(solution)/shard_map/ppermute | solution.py:294
  54.3 19.2 %collective-permute-start.11 = (bf16[64,4096]{1,0:T(8,128)(2,1)}, bf16[64,4096]{1,0:T(8,128)(2,1)}, u32[]{:S(2)}, u32[]{:S(2)}) collective-permute-start(bf16[64,4096]{1,0:T(8,128)(2,1)} %fusion.4), channel_id=1, source_target_pairs={{24,16},{16,8},{25,17},{17,9},{26,18},{18,10},{27,19},{19,11},{28,... | collective-permute-start | bytes 1572872 | tf_op jit(solution)/shard_map/ppermute | solution.py:295
  58.9 14.6 %copy-start.3 = (bf16[4,64,4096]{2,1,0:T(8,128)(2,1)S(1)}, bf16[4,64,4096]{2,1,0:T(8,128)(2,1)}, u32[]{:S(2)}) copy-start(bf16[4,64,4096]{2,1,0:T(8,128)(2,1)} %get-tuple-element.23) | copy-start | bytes 6291460
  63.4 17.4 %collective-permute-start.4 = (bf16[64,4096]{1,0:T(8,128)(2,1)S(1)}, bf16[64,4096]{1,0:T(8,128)(2,1)S(1)}, u32[]{:S(2)}, u32[]{:S(2)}) collective-permute-start(bf16[64,4096]{1,0:T(8,128)(2,1)S(1)} %fusion.7), channel_id=1, source_target_pairs={{0,8},{8,16},{1,9},{9,17},{2,10},{10,18},{3,11},{11,19},{4,12},{12... | collective-permute-start | bytes 1572872 | tf_op jit(solution)/shard_map/ppermute | solution.py:294
  64.7 19.9 %collective-permute-start.6 = (bf16[64,4096]{1,0:T(8,128)(2,1)S(1)}, bf16[64,4096]{1,0:T(8,128)(2,1)S(1)}, u32[]{:S(2)}, u32[]{:S(2)}) collective-permute-start(bf16[64,4096]{1,0:T(8,128)(2,1)S(1)} %fusion.7), channel_id=1, source_target_pairs={{24,16},{16,8},{25,17},{17,9},{26,18},{18,10},{27,19},{19,11},{28,... | collective-permute-start | bytes 1572872 | tf_op jit(solution)/shard_map/ppermute | solution.py:295
  74.9 20.9 %collective-permute-start.12 = (bf16[64,4096]{1,0:T(8,128)(2,1)S(1)}, bf16[64,4096]{1,0:T(8,128)(2,1)S(1)}, u32[]{:S(2)}, u32[]{:S(2)}) collective-permute-start(bf16[64,4096]{1,0:T(8,128)(2,1)S(1)} %get-tuple-element.28), channel_id=1, source_target_pairs={{24,16},{16,8},{8,0},{25,17},{17,9},{9,1},{26,18},{18,10},{10,2},{... | collective-permute-start | bytes 1572872 | tf_op jit(solution)/shard_map/ppermute | solution.py:295
  77.0 18.8 %collective-permute-start.10 = (bf16[64,4096]{1,0:T(8,128)(2,1)S(1)}, bf16[64,4096]{1,0:T(8,128)(2,1)S(1)}, u32[]{:S(2)}, u32[]{:S(2)}) collective-permute-start(bf16[64,4096]{1,0:T(8,128)(2,1)S(1)} %get-tuple-element.27), channel_id=1, source_target_pairs={{0,8},{8,16},{16,24},{1,9},{9,17},{17,25},{2,10},{10,18},{18,26},{... | collective-permute-start | bytes 1572872 | tf_op jit(solution)/shard_map/ppermute | solution.py:294
  84.9 21.7 %collective-permute-start.7 = (bf16[64,4096]{1,0:T(8,128)(2,1)S(1)}, bf16[64,4096]{1,0:T(8,128)(2,1)S(1)}, u32[]{:S(2)}, u32[]{:S(2)}) collective-permute-start(bf16[64,4096]{1,0:T(8,128)(2,1)S(1)} %get-tuple-element.26), channel_id=1, source_target_pairs={{24,16},{16,8},{8,0},{25,17},{17,9},{9,1},{26,18},{18,10},{10,2},{... | collective-permute-start | bytes 1572872 | tf_op jit(solution)/shard_map/ppermute | solution.py:295
  87.0 19.8 %copy-start.8 = (s32[1,4096]{1,0:T(1,128)S(1)}, s32[1,4096]{1,0:T(1,128)}, u32[]{:S(2)}) copy-start(s32[1,4096]{1,0:T(1,128)} %param.23) | copy-start | bytes 49156
  87.0 19.8 %copy-start.10 = (s32[128]{0:T(128)S(1)}, s32[128]{0:T(128)}, u32[]{:S(2)}) copy-start(s32[128]{0:T(128)} %param.22) | copy-start | bytes 1540
  87.0 19.6 %collective-permute-start.5 = (bf16[64,4096]{1,0:T(8,128)(2,1)S(1)}, bf16[64,4096]{1,0:T(8,128)(2,1)S(1)}, u32[]{:S(2)}, u32[]{:S(2)}) collective-permute-start(bf16[64,4096]{1,0:T(8,128)(2,1)S(1)} %get-tuple-element.25), channel_id=1, source_target_pairs={{0,8},{8,16},{16,24},{1,9},{9,17},{17,25},{2,10},{10,18},{18,26},{... | collective-permute-start | bytes 1572872 | tf_op jit(solution)/shard_map/ppermute | solution.py:294
  (1 other events, 0.8 us)
Sparse Core Ops, SparseCore 0:
  19.3 39.5 all-gather.1
